TPU v7x, 512 devices: a whole 4x8x8 slice. The times are simulated.
512 devices in a mesh: tile: 128 (over z, x, y_lo), cls: 4 (over y_hi, core).
Axes of the slice: x: 4, y: 8 (y_hi: 2, y_lo: 4; y = y_hi * 4 + y_lo), z: 8, core: 2. Of those that a mesh axis runs over, the one named last changes fastest.
Arguments:
- concentration: float32 [64, 4, 262144], P('cls', None, 'tile'), may hold values from 0.05 to 2
- velocity: float32 [2, 4, 262144], P(None, None, 'tile'), may hold values from -0.3 to 0.3
- land_mask: int32 [262144], P('tile'), may hold values 0 or 1
- settling: float32 [64], P('cls'), may hold values from 0.01 to 0.3
- breakage_rate: float32 [64], replicated, may hold values from 0.02 to 0.3
- kernel_levels: int32 [64, 64], replicated, may hold values from 100 to 1000, as said below
- pair_target: int32 [64, 64], replicated, may hold values from 0 to 63, as said below
- fragment_weights: int32 [64, 64], replicated, may hold values from 1 to 16
Outputs:
- flocs: float32 [64, 4, 262144], P('cls', None, 'tile')
Inputs may be any that keep to these rules, and one draw needn't show every extreme that they name: `kernel_levels`: symmetric. `pair_target`: symmetric, and entry [i, j] is at least the larger of i and j.
All inputs are finite; a program needn't handle non-finite values. No bound on the sum of `land_mask` on one device may be relied on, other than what follows from the above.
Results may differ from a plain program's by a relative error of at most 0.0001.
Values sent between devices are 32-bit elements; how exact they have to be, the bound alone decides.
No kernel may reach another device: no remote copies, remote signals or barrier semaphores. Data moves between devices by JAX's collectives and lax.ppermute only.
A program may use at most 64 MiB of HBM per device.

v0:
```python
import jax
import jax.numpy as jnp
from jax import lax
from jax.sharding import Mesh
from jax.sharding import PartitionSpec as P

CY = 512
CX = 4
CLS = ("cls_0", "cls_1")


kernel_scale = 1e-05
temp_floats = 2097152


def passed_along(x, axis, by):
    length = lax.axis_size(axis)
    pairs = [(i, i + by) for i in range(length) if 0 <= i + by < length]
    return lax.ppermute(x, axis, pairs)


def sent_to_all(x, axis):
    length = lax.axis_size(axis)
    return lax.all_to_all(jnp.broadcast_to(x[None], (length, *x.shape)), axis, 0, 0, tiled=True)


def in_order(tiles, dim):
    shape = list(tiles.shape[1:])
    shape[dim] *= tiles.shape[0]
    return jnp.moveaxis(tiles, 0, dim).reshape(shape)


def whole_of(x, axes, dim):
    far, near = axes
    leading = sent_to_all(x, far)
    tiles = jnp.swapaxes(sent_to_all(leading, near), 0, 1)
    return in_order(tiles.reshape(-1, *x.shape), dim)


def face_flux(low, high, group, part):
    speed = 0.5 * (low[group + part] + high[group + part]) * low[group + 2] * high[group + 2]
    return jnp.maximum(speed, 0.0) * low[:group] + jnp.minimum(speed, 0.0) * high[:group]


def make_tables(start, count, kernel_levels, pair_target, fragment_weights, breakage_rate):
    total = kernel_levels.shape[0]
    levels = kernel_levels.astype(jnp.float32) * kernel_scale
    rank = jnp.arange(total, dtype=jnp.int32)
    mine = start + jnp.arange(count, dtype=jnp.int32)
    hit = pair_target[None, :, :] == mine[:, None, None]
    birth = jnp.where(hit, 0.5 * levels[None, :, :], 0.0)
    pairs = jnp.transpose(birth, (1, 0, 2)).reshape(total * count, total)
    lower = jnp.where(rank[:, None] <= rank[None, :], fragment_weights.astype(jnp.float32), 0.0)
    frag = lower / jnp.sum(lower, axis=0, keepdims=True)
    kernel_rows = lax.dynamic_slice_in_dim(levels, start, count, 0)
    frag_rows = lax.dynamic_slice_in_dim(frag, start, count, 0)
    rate_rows = lax.dynamic_slice_in_dim(breakage_rate, start, count, 0)
    return (pairs, kernel_rows, frag_rows, rate_rows)


def react(own, whole, tables, breakage_rate):
    pairs, kernel_rows, frag_rows, rate_rows = tables
    count, width = own.shape
    total = whole.shape[0]
    block = max(1, min(width, temp_floats // (total * count)))
    while width % block != 0:
        block = block - 1
    steps_count = width // block

    def add_block(index, gain):
        offset = index * block
        cols = lax.dynamic_slice_in_dim(whole, offset, block, 1)
        made = jnp.dot(
            pairs, cols, precision=lax.Precision.HIGHEST, preferred_element_type=jnp.float32
        )
        part_gain = jnp.sum(made.reshape(total, count, block) * cols[:, None, :], axis=0)
        return lax.dynamic_update_slice_in_dim(gain, part_gain, offset, 1)

    gain = lax.fori_loop(0, steps_count, add_block, jnp.zeros((count, width), jnp.float32))
    loss = own * jnp.dot(
        kernel_rows, whole, precision=lax.Precision.HIGHEST, preferred_element_type=jnp.float32
    )
    broken = (
        jnp.dot(
            frag_rows,
            breakage_rate[:, None] * whole,
            precision=lax.Precision.HIGHEST,
            preferred_element_type=jnp.float32,
        )
        - rate_rows[:, None] * own
    )
    return own + gain - loss + broken


def body(
    concentration,
    velocity,
    land_mask,
    settling,
    breakage_rate,
    kernel_levels,
    pair_target,
    fragment_weights,
):
    group, layers, columns = concentration.shape
    field = concentration.reshape(group, layers, CX, CY)
    water = land_mask.astype(jnp.float32).reshape(1, 1, CX, CY)
    stacked = jnp.concatenate(
        [field, velocity.reshape(2, layers, CX, CY), jnp.broadcast_to(water, (1, layers, CX, CY))],
        0,
    )
    west = passed_along(stacked[:, :, CX - 1 :, :], "tile", 1)
    east = passed_along(stacked[:, :, :1, :], "tile", -1)
    along_x = jnp.concatenate([west, stacked, east], 2)
    along_y = jnp.pad(stacked, ((0, 0), (0, 0), (0, 0), (1, 1)))
    flux_x = face_flux(along_x[:, :, :-1], along_x[:, :, 1:], group, 0)
    flux_y = face_flux(along_y[:, :, :, :-1], along_y[:, :, :, 1:], group, 1)
    moved = (
        field
        - (flux_x[:, :, 1:] - flux_x[:, :, :-1])
        - (flux_y[:, :, :, 1:] - flux_y[:, :, :, :-1])
    )
    sink = settling[:, None, None, None] * field
    moved = moved - sink + jnp.pad(sink[:, :-1], ((0, 0), (1, 0), (0, 0), (0, 0)))
    current = moved.reshape(group, layers * columns)
    start = lax.axis_index(CLS) * group
    tables = make_tables(start, group, kernel_levels, pair_target, fragment_weights, breakage_rate)
    for sub in range(2):
        whole = whole_of(current, ("cls_0", "cls_1"), 0)
        current = react(current, whole, tables, breakage_rate)
    return current.reshape(group, layers, columns)


def solution(mesh):
    finer = Mesh(mesh.devices.reshape(mesh.shape["tile"], 2, 2), ("tile", "cls_0", "cls_1"))
    placed = (P(CLS, None, "tile"), P(None, None, "tile"), P("tile"), P(CLS), P(), P(), P(), P())
    return jax.shard_map(
        body, mesh=finer, in_specs=placed, out_specs=P(CLS, None, "tile"), check_vma=False
    )
```

profile of v0, /device:TPU:7, one launch (start us, length us, event | category | flops | bytes accessed | tf_op | source)
XLA Modules:
  0.0 172.8 jit_solution(5752832472238718000)
XLA Ops:
  0.0 1.5 reshape.51
  3.6 3.2 %collective-permute-start = (f32[19,4,1,512]{3,2,1,0:T(1,128)S(1)}, f32[19,4,1,512]{3,2,1,0:T(1,128)S(1)}, u32[]{:S(2)}, u32[]{:S(2)}) collective-permute-start(f32[19,4,1,512]{3,2,1,0:T(1,128)S(1)} %get-tuple-element.227), channel_id=1, source_target_pairs={{0,4},{4,8},{8,12},{12,16},{16,20},{20,24},{24,28},{28,32},{32,36}... | collective-permute-start | bytes 466952 | tf_op jit(solution)/shard_map/ppermute | solution.py:19
  6.8 4.8 %collective-permute-start.1 = (f32[19,4,1,512]{3,2,1,0:T(1,128)S(1)}, f32[19,4,1,512]{3,2,1,0:T(1,128)S(1)}, u32[]{:S(2)}, u32[]{:S(2)}) collective-permute-start(f32[19,4,1,512]{3,2,1,0:T(1,128)S(1)} %get-tuple-element.228), channel_id=1, source_target_pairs={{4,0},{8,4},{12,8},{16,12},{20,16},{24,20},{28,24},{32,28},{36,32}... | collective-permute-start | bytes 466952 | tf_op jit(solution)/shard_map/ppermute | solution.py:19
  13.1 4.5 %collective-permute-done.1 = f32[19,4,1,512]{3,2,1,0:T(1,128)S(1)} collective-permute-done((f32[19,4,1,512]{3,2,1,0:T(1,128)S(1)}, f32[19,4,1,512]{3,2,1,0:T(1,128)S(1)}, u32[]{:S(2)}, u32[]{:S(2)}) %collective-permute-start.1) | collective-permute-done | bytes 155680 | tf_op jit(solution)/shard_map/ppermute | solution.py:19
  20.2 4.6 %all-to-all-start = ((f32[2,16,8192]{2,1,0:T(8,128)}), f32[2,16,8192]{2,1,0:T(8,128)S(1)}, u32[]{:S(2)}, u32[]{:S(2)}) async-start(f32[2,16,8192]{2,1,0:T(8,128)} %broadcast_in_dim.37), calls=%async_computation | async-start | bytes 2097152 | tf_op jit(solution)/shard_map/all_to_all | solution.py:24
  25.0 15.1 %all-to-all-done = f32[2,16,8192]{2,1,0:T(8,128)S(1)} async-done(((f32[2,16,8192]{2,1,0:T(8,128)}), f32[2,16,8192]{2,1,0:T(8,128)S(1)}, u32[]{:S(2)}, u32[]{:S(2)}) %all-to-all-start) | async-done | bytes 1048608 | tf_op jit(solution)/shard_map/all_to_all | solution.py:24
  40.3 19.5 %all_to_all.20 = f32[2,2,16,8192]{3,2,1,0:T(8,128)S(1)} all-to-all(f32[2,2,16,8192]{3,2,1,0:T(8,128)S(1)} %broadcast_in_dim.38), channel_id=1, replica_groups=mesh['tile'=128,'cls_0'=2,'cls_1'=2] {'cls_1'}, dimensions={0} | all-to-all | bytes 4194304 | tf_op jit(solution)/shard_map/all_to_all | solution.py:24
  60.5 33.4 %while.28 = (s32[]{:T(128)}, f32[16,8192]{1,0:T(8,128)S(1)}, f32[64,8192]{1,0:T(8,128)S(1)}, s32[64,64]{1,0:T(8,128)S(1)}, s32[1024]{0:T(1024)S(1)}, /*index=5*/...) while((s32[]{:T(128)}, f32[16,8192]{1,0:T(8,128)S(1)}, ...), condition=%wide.region_2.3_spmd.clone, body=%wide.region_0.2_spmd.clone.sunk | while | flops 1614905344 | bytes 19828892 | solution.py:79
  60.8 6.7 %fusion.53 = f32[2048,1024]{0,1:T(8,128)S(1)} fusion(f32[64,2048]{1,0:T(8,128)S(1)} %constant_dynamic-slice_fusion.4, f32[1024,64]{1,0:T(8,128)S(1)} %bitcast_select_fusion.4), kind=kOutput, calls=%fused_computation.77.clone.1 | convolution fusion | flops 1610612736 | bytes 9175040 | tf_op jit(solution)/shard_map/while/body/eval_jaxpr/dot_general | solution.py:73
  67.5 1.4 multiply_reduce_fusion.4
  69.1 6.7 %fusion.53 = f32[2048,1024]{0,1:T(8,128)S(1)} fusion(f32[64,2048]{1,0:T(8,128)S(1)} %constant_dynamic-slice_fusion.4, f32[1024,64]{1,0:T(8,128)S(1)} %bitcast_select_fusion.4), kind=kOutput, calls=%fused_computation.77.clone.1 | convolution fusion | flops 1610612736 | bytes 9175040 | tf_op jit(solution)/shard_map/while/body/eval_jaxpr/dot_general | solution.py:73
  75.8 1.4 multiply_reduce_fusion.4
  77.5 6.7 %fusion.53 = f32[2048,1024]{0,1:T(8,128)S(1)} fusion(f32[64,2048]{1,0:T(8,128)S(1)} %constant_dynamic-slice_fusion.4, f32[1024,64]{1,0:T(8,128)S(1)} %bitcast_select_fusion.4), kind=kOutput, calls=%fused_computation.77.clone.1 | convolution fusion | flops 1610612736 | bytes 9175040 | tf_op jit(solution)/shard_map/while/body/eval_jaxpr/dot_general | solution.py:73
  84.2 1.4 multiply_reduce_fusion.4
  85.8 6.7 %fusion.53 = f32[2048,1024]{0,1:T(8,128)S(1)} fusion(f32[64,2048]{1,0:T(8,128)S(1)} %constant_dynamic-slice_fusion.4, f32[1024,64]{1,0:T(8,128)S(1)} %bitcast_select_fusion.4), kind=kOutput, calls=%fused_computation.77.clone.1 | convolution fusion | flops 1610612736 | bytes 9175040 | tf_op jit(solution)/shard_map/while/body/eval_jaxpr/dot_general | solution.py:73
  92.5 1.4 multiply_reduce_fusion.4
  97.3 3.6 %all-to-all-start.2 = ((f32[2,16,8192]{2,1,0:T(8,128)}), f32[2,16,8192]{2,1,0:T(8,128)S(1)}, u32[]{:S(2)}, u32[]{:S(2)}) async-start(f32[2,16,8192]{2,1,0:T(8,128)} %broadcast_in_dim.43), calls=%async_computation.2 | async-start | bytes 2097152 | tf_op jit(solution)/shard_map/all_to_all | solution.py:24
  100.9 17.7 %all-to-all-done.2 = f32[2,16,8192]{2,1,0:T(8,128)S(1)} async-done(((f32[2,16,8192]{2,1,0:T(8,128)}), f32[2,16,8192]{2,1,0:T(8,128)S(1)}, u32[]{:S(2)}, u32[]{:S(2)}) %all-to-all-start.2) | async-done | bytes 1048608 | tf_op jit(solution)/shard_map/all_to_all | solution.py:24
  118.7 17.0 %all_to_all.21 = f32[2,2,16,8192]{3,2,1,0:T(8,128)S(1)} all-to-all(f32[2,2,16,8192]{3,2,1,0:T(8,128)S(1)} %broadcast_in_dim.45), channel_id=1, replica_groups=mesh['tile'=128,'cls_0'=2,'cls_1'=2] {'cls_1'}, dimensions={0} | all-to-all | bytes 4194304 | tf_op jit(solution)/shard_map/all_to_all | solution.py:24
  135.9 33.4 %while.29 = (s32[]{:T(128)}, f32[16,8192]{1,0:T(8,128)S(1)}, f32[64,8192]{1,0:T(8,128)S(1)}, s32[64,64]{1,0:T(8,128)S(1)}, s32[1024]{0:T(1024)S(1)}, /*index=5*/...) while((s32[]{:T(128)}, f32[16,8192]{1,0:T(8,128)S(1)}, ...), condition=%wide.region_6.7_spmd.clone, body=%wide.region_4.6_spmd.clone.sunk | while | flops 1614905344 | bytes 19828892 | solution.py:79
  136.1 6.7 %fusion.56 = f32[2048,1024]{0,1:T(8,128)S(1)} fusion(f32[64,2048]{1,0:T(8,128)S(1)} %constant_dynamic-slice_fusion.5, f32[1024,64]{1,0:T(8,128)S(1)} %bitcast_select_fusion.5), kind=kOutput, calls=%fused_computation.78.clone.1 | convolution fusion | flops 1610612736 | bytes 9175040 | tf_op jit(solution)/shard_map/while/body/eval_jaxpr/dot_general | solution.py:73
  144.5 6.7 %fusion.56 = f32[2048,1024]{0,1:T(8,128)S(1)} fusion(f32[64,2048]{1,0:T(8,128)S(1)} %constant_dynamic-slice_fusion.5, f32[1024,64]{1,0:T(8,128)S(1)} %bitcast_select_fusion.5), kind=kOutput, calls=%fused_computation.78.clone.1 | convolution fusion | flops 1610612736 | bytes 9175040 | tf_op jit(solution)/shard_map/while/body/eval_jaxpr/dot_general | solution.py:73
  152.9 6.7 %fusion.56 = f32[2048,1024]{0,1:T(8,128)S(1)} fusion(f32[64,2048]{1,0:T(8,128)S(1)} %constant_dynamic-slice_fusion.5, f32[1024,64]{1,0:T(8,128)S(1)} %bitcast_select_fusion.5), kind=kOutput, calls=%fused_computation.78.clone.1 | convolution fusion | flops 1610612736 | bytes 9175040 | tf_op jit(solution)/shard_map/while/body/eval_jaxpr/dot_general | solution.py:73
  161.2 6.7 %fusion.56 = f32[2048,1024]{0,1:T(8,128)S(1)} fusion(f32[64,2048]{1,0:T(8,128)S(1)} %constant_dynamic-slice_fusion.5, f32[1024,64]{1,0:T(8,128)S(1)} %bitcast_select_fusion.5), kind=kOutput, calls=%fused_computation.78.clone.1 | convolution fusion | flops 1610612736 | bytes 9175040 | tf_op jit(solution)/shard_map/while/body/eval_jaxpr/dot_general | solution.py:73
  (75 shorter events, 21.8 us)
Async XLA Ops:
  0.0 11.7 %copy-start.4 = (f32[16]{0:T(128)S(1)}, f32[16]{0:T(128)}, u32[]{:S(2)}) copy-start(f32[16]{0:T(128)} %param.15) | copy-start | bytes 196
  3.6 9.5 %collective-permute-start = (f32[19,4,1,512]{3,2,1,0:T(1,128)S(1)}, f32[19,4,1,512]{3,2,1,0:T(1,128)S(1)}, u32[]{:S(2)}, u32[]{:S(2)}) collective-permute-start(f32[19,4,1,512]{3,2,1,0:T(1,128)S(1)} %get-tuple-element.227), channel_id=1, source_target_pairs={{0,4},{4,8},{8,12},{12,16},{16,20},{20,24},{24,28},{28,32},{32,36}... | collective-permute-start | bytes 466952 | tf_op jit(solution)/shard_map/ppermute | solution.py:19
  6.8 10.8 %collective-permute-start.1 = (f32[19,4,1,512]{3,2,1,0:T(1,128)S(1)}, f32[19,4,1,512]{3,2,1,0:T(1,128)S(1)}, u32[]{:S(2)}, u32[]{:S(2)}) collective-permute-start(f32[19,4,1,512]{3,2,1,0:T(1,128)S(1)} %get-tuple-element.228), channel_id=1, source_target_pairs={{4,0},{8,4},{12,8},{16,12},{20,16},{24,20},{28,24},{32,28},{36,32}... | collective-permute-start | bytes 466952 | tf_op jit(solution)/shard_map/ppermute | solution.py:19
  19.1 5.8 %copy-start.1 = (s32[64,64]{1,0:T(8,128)S(1)}, s32[64,64]{1,0:T(8,128)}, u32[]{:S(2)}) copy-start(s32[64,64]{1,0:T(8,128)} %param.17) | copy-start | bytes 49156
  19.2 5.8 %copy-start.3 = (f32[64]{0:T(128)S(1)}, f32[64]{0:T(128)}, u32[]{:S(2)}) copy-start(f32[64]{0:T(128)} %param.16) | copy-start | bytes 772
  19.2 5.9 %copy-start.2 = (s32[64,64]{1,0:T(8,128)S(1)}, s32[64,64]{1,0:T(8,128)}, u32[]{:S(2)}) copy-start(s32[64,64]{1,0:T(8,128)} %param.19) | copy-start | bytes 49156
  20.2 19.9 %all-to-all-start = ((f32[2,16,8192]{2,1,0:T(8,128)}), f32[2,16,8192]{2,1,0:T(8,128)S(1)}, u32[]{:S(2)}, u32[]{:S(2)}) async-start(f32[2,16,8192]{2,1,0:T(8,128)} %broadcast_in_dim.37), calls=%async_computation | async-start | bytes 2097152 | tf_op jit(solution)/shard_map/all_to_all | solution.py:24
  59.8 0.8 copy-start
  97.3 21.2 %all-to-all-start.2 = ((f32[2,16,8192]{2,1,0:T(8,128)}), f32[2,16,8192]{2,1,0:T(8,128)S(1)}, u32[]{:S(2)}, u32[]{:S(2)}) async-start(f32[2,16,8192]{2,1,0:T(8,128)} %broadcast_in_dim.43), calls=%async_computation.2 | async-start | bytes 2097152 | tf_op jit(solution)/shard_map/all_to_all | solution.py:24
where the time goes:
time: 174 us; the launch traced here: 173 us
  matrix products  58.1 us (33%)
  waiting for transfers between devices  38 us (22%)
  blocking collectives  36.5 us (21%)
  starting transfers between devices  16.2 us (9%)
  other arithmetic  15.3 us (9%)
  local copies, waits for them, and re-layouts  8.08 us (5%)
    dot_general x8, matrix products, add_block(): jnp.dot(pairs, cols, precision=lax.Precision.HIGHEST, preferred_element_t...  53.4 us
    all_to_all x2, blocking collectives, sent_to_all(): lax.all_to_all(jnp.broadcast_to(x[None], (length, *x.shape)), axis, 0, 0,...  36.5 us
    all_to_all x2, waiting for transfers between devices, sent_to_all(): lax.all_to_all(jnp.broadcast_to(x[None], (length, *x.shape)), axis, 0, 0,...  32.7 us
    reduce_sum x8, other arithmetic, add_block(): jnp.sum(made.reshape(total, count, block) * cols[:, None, :], axis=0)  10.9 us
    all_to_all x2, starting transfers between devices, sent_to_all(): lax.all_to_all(jnp.broadcast_to(x[None], (length, *x.shape)), axis, 0, 0,...  8.19 us
    ppermute x2, starting transfers between devices, passed_along(): return lax.ppermute(x, axis, pairs)  7.98 us
    ppermute x2, waiting for transfers between devices, passed_along(): return lax.ppermute(x, axis, pairs)  5.27 us
  transfers between devices with their start and end apart: 4, of which 4 were waited for; matrix products, arithmetic and copies ran while one was open for 1% of the time, Pallas kernels for 0%

commit v1 on v0

v1 whole, which is shorter than its diff:
```python
import jax
import jax.numpy as jnp
from jax import lax
from jax.experimental import pallas as pl
from jax.experimental.pallas import tpu as pltpu
from jax.sharding import PartitionSpec as P

CY = 512
CX = 4
LAYERS = 4
NC = 64
GROUP = 16
COLS = CX * CY
TILE = 256
HALF_SCALE = 0.5e-05
VMEM_LIMIT = 48 * 1024 * 1024

SPANS = [NC - 8 * b for b in range(NC // 8)]
STARTS = [8 * sum(SPANS[:b]) for b in range(NC // 8)]
PAIR_ROWS = 8 * sum(SPANS)


def split(x):
    high = x.astype(jnp.bfloat16)
    low = (x - high.astype(jnp.float32)).astype(jnp.bfloat16)
    return high, low


def table_kernel(levels_ref, target_ref, weights_ref, rate_ref, pair_ref, linear_ref):
    levels = levels_ref[...].astype(jnp.float32)
    row = lax.broadcasted_iota(jnp.int32, (NC, NC), 0)
    col = lax.broadcasted_iota(jnp.int32, (NC, NC), 1)
    double = 2.0 * levels
    high, low = [part.astype(jnp.float32) for part in split(double)]
    weight = jnp.where(col < row, 1.0, jnp.where(col == row, 0.5, 0.0))
    lost = jnp.concatenate([high, high, low, low], 1)
    born = lost * jnp.concatenate([weight] * 4, 1)
    target = jnp.concatenate([target_ref[...]] * 4, 1)
    for b in range(NC // 8):
        span = SPANS[b]
        klass = lax.broadcasted_iota(jnp.int32, (span, 4 * NC), 0) + 8 * b
        for two in range(4):
            rows = []
            for i in (8 * b + 2 * two, 8 * b + 2 * two + 1):
                gain = jnp.where(klass == target[i : i + 1], born[i : i + 1], 0.0)
                loss = jnp.where(klass == i, lost[i : i + 1], 0.0)
                rows.append(gain - loss)
            at = STARTS[b] + 2 * two * span
            pair_ref[at : at + 2 * span, :] = jnp.concatenate(rows, 0).astype(jnp.bfloat16)
    lower = jnp.where(row <= col, weights_ref[...].astype(jnp.float32), 0.0)
    rate = rate_ref[...]
    linear = lower / jnp.sum(lower, axis=0, keepdims=True) * rate
    linear = linear - jnp.where(row == col, rate, 0.0)
    high, low = split(linear)
    linear_ref[...] = jnp.concatenate([high, high, low, low], 1)


def make_tables(kernel_levels, pair_target, fragment_weights, breakage_rate):
    return pl.pallas_call(
        table_kernel,
        out_shape=(
            jax.ShapeDtypeStruct((PAIR_ROWS, 4 * NC), jnp.bfloat16),
            jax.ShapeDtypeStruct((NC, 4 * NC), jnp.bfloat16),
        ),
        compiler_params=pltpu.CompilerParams(vmem_limit_bytes=VMEM_LIMIT),
        name="tables",
    )(kernel_levels, pair_target, fragment_weights, breakage_rate.reshape(1, NC))


def transport_kernel(
    c_ref, velocity_ref, mask_ref, settling_ref, west_ref, east_ref, out_ref
):
    mask = mask_ref[...].astype(jnp.float32)
    water = jnp.concatenate([mask[q : q + 1] for q in range(COLS // 128)], 1)
    wide = jnp.concatenate(
        [west_ref[GROUP + 1, 0:1, :], water, east_ref[GROUP + 1, 0:1, :]], 1
    )
    both_x = 0.5 * wide[:, :-CY] * wide[:, CY:]
    place = lax.broadcasted_iota(jnp.int32, (1, COLS), 1)
    both_y = jnp.where(place % CY == 0, 0.0, 0.5 * water * pltpu.roll(water, 1, 1))
    eye = lax.broadcasted_iota(jnp.int32, (GROUP, GROUP), 0) == lax.broadcasted_iota(
        jnp.int32, (GROUP, GROUP), 1
    )
    sink = jnp.sum(jnp.where(eye, settling_ref[...], 0.0), axis=1, keepdims=True)
    above = None
    for layer in range(LAYERS):
        c = c_ref[:, layer, :]
        u = jnp.concatenate(
            [
                west_ref[GROUP, layer : layer + 1, :],
                velocity_ref[0, layer : layer + 1, :],
                east_ref[GROUP, layer : layer + 1, :],
            ],
            1,
        )
        face_x = (u[:, :-CY] + u[:, CY:]) * both_x
        plus_x, minus_x = jnp.maximum(face_x, 0.0), jnp.minimum(face_x, 0.0)
        v = velocity_ref[1, layer : layer + 1, :]
        face_y = (v + pltpu.roll(v, 1, 1)) * both_y
        plus_y, minus_y = jnp.maximum(face_y, 0.0), jnp.minimum(face_y, 0.0)
        to_north = pltpu.roll(plus_y, COLS - 1, 1)
        from_north = pltpu.roll(minus_y, COLS - 1, 1)
        keep = 1.0 - plus_x[:, CY:] + minus_x[:, :-CY] - to_north + minus_y
        west = jnp.concatenate([west_ref[:GROUP, layer, :], c[:, :-CY]], 1)
        east = jnp.concatenate([c[:, CY:], east_ref[:GROUP, layer, :]], 1)
        south = pltpu.roll(c, 1, 1)
        north = pltpu.roll(c, COLS - 1, 1)
        moved = (
            c * (keep - sink)
            + west * plus_x[:, :-CY]
            - east * minus_x[:, CY:]
            + south * plus_y
            - north * from_north
        )
        if above is not None:
            moved = moved + sink * above
        above = c
        out_ref[layer] = moved


def transport(concentration, velocity, land_mask, settling, west, east):
    return pl.pallas_call(
        transport_kernel,
        out_shape=jax.ShapeDtypeStruct((LAYERS, GROUP, COLS), jnp.float32),
        compiler_params=pltpu.CompilerParams(vmem_limit_bytes=VMEM_LIMIT),
        name="transport",
    )(
        concentration,
        velocity,
        land_mask.reshape(COLS // 128, 128),
        settling.reshape(1, GROUP),
        west,
        east,
    )


def react_kernel(x_ref, pair_ref, linear_ref, out_ref):
    width = x_ref.shape[1]

    def tile(index, carry):
        at = pl.ds(pl.multiple_of(index * TILE, TILE), TILE)
        n = x_ref[:, at]
        for _ in range(2):
            high, low = split(n)
            stack = jnp.concatenate([high, low, high, low], 0)
            total = [jnp.zeros((8, TILE), jnp.float32) for _ in range(NC // 8)]
            for b in range(NC // 8):
                span = SPANS[b]
                made = jnp.dot(
                    pair_ref[STARTS[b] : STARTS[b] + 8 * span, :],
                    stack,
                    preferred_element_type=jnp.float32,
                )
                for ii in range(8):
                    partner = n[8 * b + ii : 8 * b + ii + 1]
                    for g in range(b, NC // 8):
                        row = ii * span + 8 * (g - b)
                        total[g] = total[g] + made[row : row + 8] * partner
            linear = jnp.dot(linear_ref[...], stack, preferred_element_type=jnp.float32)
            n = n + (HALF_SCALE * jnp.concatenate(total, 0) + linear)
        out_ref[:, at] = n
        return carry

    lax.fori_loop(0, width // TILE, tile, 0)


def react(x, pairs, linear):
    return pl.pallas_call(
        react_kernel,
        out_shape=jax.ShapeDtypeStruct(x.shape, jnp.float32),
        compiler_params=pltpu.CompilerParams(vmem_limit_bytes=VMEM_LIMIT),
        name="react",
    )(x, pairs, linear)


def passed_along(x, by):
    length = lax.axis_size("tile")
    pairs = [(i, i + by) for i in range(length) if 0 <= i + by < length]
    return lax.ppermute(x, "tile", pairs)


def body(
    concentration,
    velocity,
    land_mask,
    settling,
    breakage_rate,
    kernel_levels,
    pair_target,
    fragment_weights,
):
    water = land_mask.astype(jnp.float32)

    def edge(at):
        cut = slice(at, at + CY)
        return jnp.concatenate(
            [
                concentration[:, :, cut],
                velocity[:1, :, cut],
                jnp.broadcast_to(water[cut], (1, LAYERS, CY)),
            ],
            0,
        )

    west = passed_along(edge(COLS - CY), 1)
    east = passed_along(edge(0), -1)
    pairs, linear = make_tables(kernel_levels, pair_target, fragment_weights, breakage_rate)
    moved = transport(concentration, velocity, land_mask, settling, west, east)
    whole = lax.all_to_all(moved, "cls", 0, 0, tiled=True).reshape(NC, COLS)
    done = react(whole, pairs, linear).reshape(LAYERS, GROUP, COLS)
    mine = lax.all_to_all(done, "cls", 0, 0, tiled=True)
    return jnp.transpose(mine, (1, 0, 2))


def solution(mesh):
    placed = (
        P("cls", None, "tile"),
        P(None, None, "tile"),
        P("tile"),
        P("cls"),
        P(),
        P(),
        P(),
        P(),
    )
    return jax.shard_map(
        body, mesh=mesh, in_specs=placed, out_specs=P("cls", None, "tile"), check_vma=False
    )
```

time: 174 us -> 72.7 us (0.42)
  the two profiles are of different devices: /device:TPU:7 before, /device:TPU:215 now
where the time goes in v1:
time: 72.7 us; the launch traced here: 72.3 us
  waiting for transfers between devices  23.7 us (33%)
  blocking collectives  20.6 us (28%)
  starting transfers between devices  13.9 us (19%)
  Pallas kernels  10.2 us (14%)
  local copies, waits for them, and re-layouts  2.89 us (4%)
  other arithmetic  0.83 us (1%)
    all_to_all x1, blocking collectives, body(): mine = lax.all_to_all(done, 'cls', 0, 0, tiled=True)  20.6 us
    all_to_all x1, waiting for transfers between devices, body(): whole = lax.all_to_all(moved, 'cls', 0, 0, tiled=True).reshape(NC, COLS)  16.5 us
    all_to_all x1, starting transfers between devices, body(): whole = lax.all_to_all(moved, 'cls', 0, 0, tiled=True).reshape(NC, COLS)  8.6 us
    pallas_call x1, Pallas kernels, react(): pl.pallas_call(react_kernel, out_shape=jax.ShapeDtypeStruct(x.shape, jnp....  8.11 us
    ppermute x2, waiting for transfers between devices, passed_along(): return lax.ppermute(x, 'tile', pairs)  7.21 us
    ppermute x2, starting transfers between devices, passed_along(): return lax.ppermute(x, 'tile', pairs)  5.28 us
    pallas_call x1, Pallas kernels, transport(): pl.pallas_call(transport_kernel, out_shape=jax.ShapeDtypeStruct((LAYERS,...  1.76 us
  transfers between devices with their start and end apart: 3, of which 3 were waited for; matrix products, arithmetic and copies ran while one was open for 0% of the time, Pallas kernels for 0%

profile of v1, /device:TPU:215, one launch (start us, length us, event | category | flops | bytes accessed | tf_op | source)
XLA Modules:
  0.0 72.3 jit_solution(10602040160014413709)
XLA Ops:
  0.0 0.0 copy-start.6
  0.0 0.8 %convert_element_type.3 = f32[2048]{0:T(1024)S(1)} convert(s32[2048]{0:T(1024)} %param.10) | non-fusion elementwise | flops 2048 | bytes 16384 | tf_op jit(solution)/shard_map/convert_element_type | solution.py:192
  0.8 0.7 fusion.1
  1.5 1.0 %fusion = (f32[16,4,512]{2,1,0:T(4,128)S(1)}, f32[16,4,512]{2,1,0:T(4,128)S(1)}) fusion(f32[16,4,2048]{2,1,0:T(4,128)} %c_ref.1), kind=kLoop, calls=%fused_computation.2 | loop fusion | bytes 524288 | tf_op jit(solution)/shard_map/slice | solution.py:198
  2.5 3.2 %collective-permute-start = (f32[18,4,512]{2,1,0:T(4,128)S(1)}, f32[18,4,512]{2,1,0:T(4,128)S(1)}, u32[]{:S(2)}, u32[]{:S(2)}) collective-permute-start(f32[18,4,512]{2,1,0:T(4,128)S(1)} %pad_maximum_fusion), channel_id=1, source_target_pairs={{0,4},{4,8},{8,12},{12,16},{16,20},{20,24},{24,28},{28,32},{32,36}... | collective-permute-start | bytes 442376 | tf_op jit(solution)/shard_map/ppermute | solution.py:179
  5.8 2.1 %collective-permute-start.1 = (f32[18,4,512]{2,1,0:T(4,128)S(1)}, f32[18,4,512]{2,1,0:T(4,128)S(1)}, u32[]{:S(2)}, u32[]{:S(2)}) collective-permute-start(f32[18,4,512]{2,1,0:T(4,128)S(1)} %pad_maximum_fusion.1), channel_id=1, source_target_pairs={{4,0},{8,4},{12,8},{16,12},{20,16},{24,20},{28,24},{32,28},{36,32}... | collective-permute-start | bytes 442376 | tf_op jit(solution)/shard_map/ppermute | solution.py:179
  7.9 1.3 %collective-permute-done.west_ref = f32[18,4,512]{2,1,0:T(4,128)S(1)} collective-permute-done((f32[18,4,512]{2,1,0:T(4,128)S(1)}, f32[18,4,512]{2,1,0:T(4,128)S(1)}, u32[]{:S(2)}, u32[]{:S(2)}) %collective-permute-start) | collective-permute-done | bytes 147488 | tf_op jit(solution)/shard_map/ppermute | solution.py:179
  9.2 6.0 %collective-permute-done.1.east_ref = f32[18,4,512]{2,1,0:T(4,128)S(1)} collective-permute-done((f32[18,4,512]{2,1,0:T(4,128)S(1)}, f32[18,4,512]{2,1,0:T(4,128)S(1)}, u32[]{:S(2)}, u32[]{:S(2)}) %collective-permute-start.1) | collective-permute-done | bytes 147488 | tf_op jit(solution)/shard_map/ppermute | solution.py:179
  15.1 0.0 copy-done.2
  15.1 0.0 copy-done.1
  15.1 0.0 copy-done
  15.1 0.0 copy-start.3
  15.1 0.0 copy-start.4
  15.2 0.0 copy-start.5
  15.2 0.0 copy-start.7
  15.2 1.8 %transport.1 = f32[4,16,2048]{2,1,0:T(8,128)} custom-call(f32[16,4,2048]{2,1,0:T(4,128)S(1)} %copy-done, f32[2,4,2048]{2,1,0:T(4,128)S(1)} %copy-done.1, s32[16,128]{1,0:T(8,128)S(1)} %bitcast.8, f32[1,16]{1,0:T(1,128)S(1)} %bitcast.9, f32[18,4,512]{2,1,0:T(4,128)S(1)} %collective-permute-done.west_ref, f32[18,4,512]{2,1,0:T(4,128)S(1)} %collective-permute-done.1.east_ref), custom_call_target="tpu_custom_call" | custom-call | tf_op jit(solution)/shard_map/transport/pallas_call | solution.py:122
  16.9 8.6 %all-to-all-start = ((f32[4,16,2048]{2,1,0:T(8,128)}), f32[4,16,2048]{2,1,0:T(8,128)S(1)}, u32[]{:S(2)}, u32[]{:S(2)}) async-start(f32[4,16,2048]{2,1,0:T(8,128)} %transport.1), calls=%async_computation | async-start | bytes 1048576 | tf_op jit(solution)/shard_map/all_to_all | solution.py:209
  25.5 0.0 copy-done.5
  25.5 0.0 copy-done.7
  25.6 0.4 tables.1
  25.9 16.5 %all-to-all-done = f32[4,16,2048]{2,1,0:T(8,128)S(1)} async-done(((f32[4,16,2048]{2,1,0:T(8,128)}), f32[4,16,2048]{2,1,0:T(8,128)S(1)}, u32[]{:S(2)}, u32[]{:S(2)}) %all-to-all-start) | async-done | bytes 524320 | tf_op jit(solution)/shard_map/all_to_all | solution.py:209
  42.4 8.1 %react.1 = f32[64,2048]{1,0:T(8,128)S(1)} custom-call(f32[64,2048]{1,0:T(8,128)S(1)} %bitcast.6, bf16[2304,256]{1,0:T(8,128)(2,1)S(1)} %get-tuple-element.7.pair_ref, bf16[64,256]{1,0:T(8,128)(2,1)S(1)} %get-tuple-element.8.linear_ref), custom_call_target="tpu_custom_call" | custom-call | tf_op jit(solution)/shard_map/react/pallas_call | solution.py:168
  50.5 20.6 %all_to_all.10 = f32[4,16,2048]{2,1,0:T(8,128)S(1)} all-to-all(f32[4,16,2048]{2,1,0:T(8,128)S(1)} %bitcast.7), channel_id=1, replica_groups=mesh['tile'=128,'cls'=4] {'cls'}, dimensions={0} | all-to-all | bytes 1048576 | tf_op jit(solution)/shard_map/all_to_all | solution.py:211
  71.2 1.1 %copy.10 = f32[16,4,2048]{2,1,0:T(4,128)} copy(f32[16,4,2048]{2,0,1:T(8,128)S(1)} %bitcast.11) | data formatting | bytes 1048576 | tf_op jit(solution)/shard_map/transpose | solution.py:212
  (11 shorter events, 0.1 us)
Async XLA Ops:
  0.0 15.1 %copy-start.2 = (s32[2048]{0:T(1024)S(1)}, s32[2048]{0:T(1024)}, u32[]{:S(2)}) copy-start(s32[2048]{0:T(1024)} %param.10) | copy-start | bytes 24580
  0.0 15.1 %copy-start.1 = (f32[2,4,2048]{2,1,0:T(4,128)S(1)}, f32[2,4,2048]{2,1,0:T(4,128)}, u32[]{:S(2)}) copy-start(f32[2,4,2048]{2,1,0:T(4,128)} %velocity_ref.1) | copy-start | bytes 196612
  0.0 15.1 %copy-start = (f32[16,4,2048]{2,1,0:T(4,128)S(1)}, f32[16,4,2048]{2,1,0:T(4,128)}, u32[]{:S(2)}) copy-start(f32[16,4,2048]{2,1,0:T(4,128)} %c_ref.1) | copy-start | bytes 1572868
  0.0 15.1 %copy-start.6 = (f32[16]{0:T(128)S(1)}, f32[16]{0:T(128)}, u32[]{:S(2)}) copy-start(f32[16]{0:T(128)} %param.11) | copy-start | bytes 196
  2.5 6.6 %collective-permute-start = (f32[18,4,512]{2,1,0:T(4,128)S(1)}, f32[18,4,512]{2,1,0:T(4,128)S(1)}, u32[]{:S(2)}, u32[]{:S(2)}) collective-permute-start(f32[18,4,512]{2,1,0:T(4,128)S(1)} %pad_maximum_fusion), channel_id=1, source_target_pairs={{0,4},{4,8},{8,12},{12,16},{16,20},{20,24},{24,28},{28,32},{32,36}... | collective-permute-start | bytes 442376 | tf_op jit(solution)/shard_map/ppermute | solution.py:179
  5.8 9.3 %collective-permute-start.1 = (f32[18,4,512]{2,1,0:T(4,128)S(1)}, f32[18,4,512]{2,1,0:T(4,128)S(1)}, u32[]{:S(2)}, u32[]{:S(2)}) collective-permute-start(f32[18,4,512]{2,1,0:T(4,128)S(1)} %pad_maximum_fusion.1), channel_id=1, source_target_pairs={{4,0},{8,4},{12,8},{16,12},{20,16},{24,20},{28,24},{32,28},{36,32}... | collective-permute-start | bytes 442376 | tf_op jit(solution)/shard_map/ppermute | solution.py:179
  15.1 10.4 %copy-start.3 = (s32[64,64]{1,0:T(8,128)S(1)}, s32[64,64]{1,0:T(8,128)}, u32[]{:S(2)}) copy-start(s32[64,64]{1,0:T(8,128)} %levels_ref.1) | copy-start | bytes 49156
  15.1 10.4 %copy-start.4 = (s32[64,64]{1,0:T(8,128)S(1)}, s32[64,64]{1,0:T(8,128)}, u32[]{:S(2)}) copy-start(s32[64,64]{1,0:T(8,128)} %target_ref.1) | copy-start | bytes 49156
  15.2 10.4 %copy-start.5 = (s32[64,64]{1,0:T(8,128)S(1)}, s32[64,64]{1,0:T(8,128)}, u32[]{:S(2)}) copy-start(s32[64,64]{1,0:T(8,128)} %weights_ref.1) | copy-start | bytes 49156
  15.2 10.4 %copy-start.7 = (f32[64]{0:T(128)S(1)}, f32[64]{0:T(128)}, u32[]{:S(2)}) copy-start(f32[64]{0:T(128)} %param.12) | copy-start | bytes 772
  16.9 25.5 %all-to-all-start = ((f32[4,16,2048]{2,1,0:T(8,128)}), f32[4,16,2048]{2,1,0:T(8,128)S(1)}, u32[]{:S(2)}, u32[]{:S(2)}) async-start(f32[4,16,2048]{2,1,0:T(8,128)} %transport.1), calls=%async_computation | async-start | bytes 1048576 | tf_op jit(solution)/shard_map/all_to_all | solution.py:209

commit v2 on v1

v2 whole, which is shorter than its diff:
```python
import jax
import jax.numpy as jnp
from jax import lax
from jax.experimental import pallas as pl
from jax.experimental.pallas import tpu as pltpu
from jax.sharding import Mesh
from jax.sharding import PartitionSpec as P

CY = 512
CX = 4
LAYERS = 4
NC = 64
GROUP = 16
COLS = CX * CY
WIDTH = 2 * CY
TILE = 256
HALF_SCALE = 0.5e-05
VMEM_LIMIT = 48 * 1024 * 1024

BLOCKS = NC // 8
ALL_SPANS = [NC - 8 * b for b in range(BLOCKS)]
OWN_SPANS = [min(NC // 2, NC - 8 * b) for b in range(BLOCKS)]


def starts(spans):
    return [8 * sum(spans[:b]) for b in range(BLOCKS + 1)]


ALL_STARTS, OWN_STARTS = starts(ALL_SPANS), starts(OWN_SPANS)


def split(x):
    high = x.astype(jnp.bfloat16)
    low = (x - high.astype(jnp.float32)).astype(jnp.bfloat16)
    return high, low


def call(kernel, out_shape, name, scratch=(), limit=VMEM_LIMIT, cost=None, **specs):
    if cost is not None:
        cost = pl.CostEstimate(flops=cost, bytes_accessed=0, transcendentals=0)
    return pl.pallas_call(
        kernel,
        out_shape=out_shape,
        scratch_shapes=scratch,
        **specs,
        compiler_params=pltpu.CompilerParams(vmem_limit_bytes=limit),
        cost_estimate=cost,
        name=name,
    )


def f32(*shape):
    return jax.ShapeDtypeStruct(shape, jnp.float32)


def table_kernel(levels_ref, target_ref, weights_ref, rate_ref, all_ref, own_ref, linear_ref):
    far = lax.axis_index("far")
    levels = levels_ref[...].astype(jnp.float32)
    row = lax.broadcasted_iota(jnp.int32, (NC, NC), 0)
    col = lax.broadcasted_iota(jnp.int32, (NC, NC), 1)
    double = 2.0 * levels
    high, low = [part.astype(jnp.float32) for part in split(double)]
    weight = jnp.where(col < row, 1.0, jnp.where(col == row, 0.5, 0.0))
    lost = jnp.concatenate([high, high, low, low], 1)
    born = lost * jnp.concatenate([weight] * 4, 1)
    target = jnp.concatenate([target_ref[...]] * 4, 1)

    def rows_of(i, first, span):
        klass = lax.broadcasted_iota(jnp.int32, (span, 4 * NC), 0) + first
        gain = jnp.where(klass == target[i : i + 1], born[i : i + 1], 0.0)
        return gain - jnp.where(klass == i, lost[i : i + 1], 0.0)

    for b in range(BLOCKS):
        for i in range(8 * b, 8 * b + 8, 2):
            span = ALL_SPANS[b]
            rows = jnp.concatenate([rows_of(i, 8 * b, span), rows_of(i + 1, 8 * b, span)], 0)
            at = ALL_STARTS[b] + (i - 8 * b) * span
            all_ref[at : at + 2 * span, :] = rows.astype(jnp.bfloat16)
            span = OWN_SPANS[b]
            first = far * (NC // 2) + (NC // 2 - span)
            rows = jnp.concatenate([rows_of(i, first, span), rows_of(i + 1, first, span)], 0)
            at = OWN_STARTS[b] + (i - 8 * b) * span
            own_ref[at : at + 2 * span, :] = rows.astype(jnp.bfloat16)
    lower = jnp.where(row <= col, weights_ref[...].astype(jnp.float32), 0.0)
    rate = rate_ref[...]
    linear = lower / jnp.sum(lower, axis=0, keepdims=True) * rate
    linear = linear - jnp.where(row == col, rate, 0.0)
    high, low = split(linear)
    linear_ref[...] = jnp.concatenate([high, high, low, low], 1)


def make_tables(kernel_levels, pair_target, fragment_weights, breakage_rate):
    bf16 = jnp.bfloat16
    return call(
        table_kernel,
        (
            jax.ShapeDtypeStruct((ALL_STARTS[-1], 4 * NC), bf16),
            jax.ShapeDtypeStruct((OWN_STARTS[-1], 4 * NC), bf16),
            jax.ShapeDtypeStruct((NC, 4 * NC), bf16),
        ),
        "tables",
    )(kernel_levels, pair_target, fragment_weights, breakage_rate.reshape(1, NC))


def column(settling):
    eye = lax.broadcasted_iota(jnp.int32, (GROUP, GROUP), 0) == lax.broadcasted_iota(
        jnp.int32, (GROUP, GROUP), 1
    )
    return jnp.sum(jnp.where(eye, settling, 0.0), axis=1, keepdims=True)


def water_of(mask_ref):
    mask = mask_ref[...].astype(jnp.float32)
    return jnp.concatenate([mask[q : q + 1] for q in range(COLS // 128)], 1)


def advect(pick, sink, out_ref):
    water_west, water, water_east = pick("water", 0)
    width = water.shape[1]
    place = lax.broadcasted_iota(jnp.int32, (1, width), 1)
    half_west = 0.5 * water_west * water
    half_east = 0.5 * water * water_east
    half_y = jnp.where(place % CY == 0, 0.0, 0.5 * water * pltpu.roll(water, 1, 1))
    above = None
    near = lax.axis_index("near")
    for layer in range(LAYERS):
        west, c, east = pick("c", layer)
        u_west, u, u_east = pick("u", layer)
        v = pick("v", layer)
        low_x = (u_west + u) * half_west
        high_x = (u + u_east) * half_east
        low_y = (v + pltpu.roll(v, 1, 1)) * half_y
        plus_y, minus_y = jnp.maximum(low_y, 0.0), jnp.minimum(low_y, 0.0)
        plus_x, minus_x = jnp.maximum(low_x, 0.0), jnp.minimum(high_x, 0.0)
        to_north = pltpu.roll(plus_y, width - 1, 1)
        from_north = pltpu.roll(minus_y, width - 1, 1)
        keep = 1.0 - jnp.maximum(high_x, 0.0) + jnp.minimum(low_x, 0.0) - to_north + minus_y
        moved = (
            c * (keep - sink)
            + west * plus_x
            - east * minus_x
            + pltpu.roll(c, 1, 1) * plus_y
            - pltpu.roll(c, width - 1, 1) * from_north
        )
        if above is not None:
            moved = moved + sink * above
        above = c
        out_ref[(near + layer // 2) % 2, layer % 2] = moved


def inner_kernel(*refs):
    taken, made = refs[:4], refs[4:7]
    here, sems = refs[7:11], refs[11]
    copies = [
        pltpu.make_async_copy(src, dst, sems.at[k]) for k, (src, dst) in enumerate(zip(taken, here))
    ]
    for copy in copies:
        copy.start()
    for copy in copies:
        copy.wait()
    inner_rows(*here, *made)


def inner_rows(c_ref, velocity_ref, mask_ref, settling_ref, out_ref, *edge_refs):
    water = water_of(mask_ref)
    even = lax.axis_index("tile") % 2 == 0

    def rows(x):
        first, last = x[..., :CY], x[..., COLS - CY :]
        return jnp.where(even, last, first), jnp.where(even, first, last)

    for ref, c, u, w in zip(edge_refs, rows(c_ref[...]), rows(velocity_ref[0]), rows(water)):
        ref[:GROUP] = c
        ref[GROUP] = u
        ref[GROUP + 1] = jnp.broadcast_to(w, (LAYERS, CY))

    def three(x):
        return x[:, : 2 * CY], x[:, CY : 3 * CY], x[:, 2 * CY :]

    def pick(what, layer):
        if what == "water":
            return three(water)
        if what == "c":
            return three(c_ref[:, layer, :])
        if what == "u":
            return three(velocity_ref[0, layer : layer + 1, :])
        return velocity_ref[1, layer : layer + 1, CY : 3 * CY]

    advect(pick, column(settling_ref[...]), out_ref)


def outer_kernel(
    c_ref,
    velocity_ref,
    mask_ref,
    settling_ref,
    even_ref,
    odd_ref,
    inner_ref,
    peer_ref,
    out_ref,
    both_ref,
):
    both_ref[0] = inner_ref[0]
    both_ref[1] = peer_ref[...]
    water = water_of(mask_ref)
    even = lax.axis_index("tile") % 2 == 0
    west_ref = jnp.where(even, odd_ref[...], even_ref[...])
    east_ref = jnp.where(even, even_ref[...], odd_ref[...])

    def three(west, x, east):
        return (
            jnp.concatenate([west, x[:, 2 * CY : 3 * CY]], 1),
            jnp.concatenate([x[:, :CY], x[:, 3 * CY :]], 1),
            jnp.concatenate([x[:, CY : 2 * CY], east], 1),
        )

    def pick(what, layer):
        if what == "water":
            return three(west_ref[GROUP + 1, :1, :], water, east_ref[GROUP + 1, :1, :])
        if what == "c":
            return three(west_ref[:GROUP, layer, :], c_ref[:, layer, :], east_ref[:GROUP, layer, :])
        if what == "u":
            at = slice(layer, layer + 1)
            return three(west_ref[GROUP, at, :], velocity_ref[0, at, :], east_ref[GROUP, at, :])
        v = velocity_ref[1, layer : layer + 1, :]
        return jnp.concatenate([v[:, :CY], v[:, 3 * CY :]], 1)

    advect(pick, column(settling_ref[...]), out_ref)


def gains(n, stack, table_ref, spans, first, count):
    total = [jnp.zeros((8, TILE), jnp.float32) for _ in range(count // 8)]
    for b in range(BLOCKS):
        span = spans[b]
        made = jnp.dot(
            table_ref[first[b] : first[b + 1], :], stack, preferred_element_type=jnp.float32
        )
        skip = (count - span) // 8
        for ii in range(8):
            partner = n[8 * b + ii : 8 * b + ii + 1]
            for g in range(span // 8):
                row = ii * span + 8 * g
                total[skip + g] = total[skip + g] + made[row : row + 8] * partner
    return jnp.concatenate(total, 0)


def stack_of(n):
    high, low = split(n)
    return jnp.concatenate([high, low, high, low], 0)


def later_react_kernel(ours_ref, theirs_ref, all_ref, own_ref, linear_ref, _, *rest):
    react_kernel(ours_ref, theirs_ref, all_ref, own_ref, linear_ref, *rest)


def react_kernel(ours_ref, theirs_ref, all_ref, own_ref, linear_ref, keep_ref, send_ref, whole):
    far, near = lax.axis_index("far"), lax.axis_index("near")
    groups = [2 * f + n for f in (far, 1 - far) for n in (near, 1 - near)]
    parts = [ref.at[place] for ref in (ours_ref, theirs_ref) for place in range(2)]

    def tile(index, carry):
        slot = index // (WIDTH // TILE)
        at = pl.ds(pl.multiple_of((index % (WIDTH // TILE)) * TILE, TILE), TILE)
        for group, part in zip(groups, parts):
            whole[group] = part[slot, :, at]
        n = whole[...].reshape(NC, TILE)
        stack = stack_of(n)
        made = gains(n, stack, all_ref, ALL_SPANS, ALL_STARTS, NC)
        linear = jnp.dot(linear_ref[...], stack, preferred_element_type=jnp.float32)
        n = n + (HALF_SCALE * made + linear)
        stack = stack_of(n)
        made = gains(n, stack, own_ref, OWN_SPANS, OWN_STARTS, NC // 2)
        mine = linear_ref[pl.ds(pl.multiple_of(far * (NC // 2), NC // 2), NC // 2), :]
        linear = jnp.dot(mine, stack, preferred_element_type=jnp.float32)
        n = jnp.where(far == 0, n[: NC // 2], n[NC // 2 :]) + (HALF_SCALE * made + linear)
        keep_ref[slot, :, at] = jnp.where(near == 0, n[:GROUP], n[GROUP:])
        send_ref[slot, :, at] = jnp.where(near == 0, n[GROUP:], n[:GROUP])
        return carry

    lax.fori_loop(0, 2 * WIDTH // TILE, tile, 0)


def react(*arrays):
    half = f32(2, GROUP, WIDTH)
    return call(
        react_kernel if len(arrays) == 5 else later_react_kernel,
        (half, half),
        "react",
        scratch=[pltpu.VMEM((4, GROUP, TILE), jnp.float32)],
        cost=8_000_000_000,
        in_specs=[pl.BlockSpec(memory_space=pltpu.VMEM)] * 5
        + [pl.BlockSpec(memory_space=pl.ANY)] * (len(arrays) - 5),
    )(*arrays)


def lay_kernel(inner_ref, outer_ref, inner_peer_ref, outer_peer_ref, out_ref):
    near = lax.axis_index("near")
    for layer in range(LAYERS):
        slot = layer % 2
        mine = near == layer // 2
        inner = jnp.where(mine, inner_ref[slot], inner_peer_ref[slot])
        outer = jnp.where(mine, outer_ref[slot], outer_peer_ref[slot])
        out_ref[:, layer, :] = jnp.concatenate([outer[:, :CY], inner, outer[:, CY:]], 1)


def swapped_in_pairs(x, first):
    length = lax.axis_size("tile")
    pairs = [(i, i + 1) for i in range(first, length - 1, 2)]
    return lax.ppermute(x, "tile", pairs + [(b, a) for a, b in pairs])


def swapped(x, axis):
    return lax.ppermute(x, axis, [(0, 1), (1, 0)])


def body(
    concentration,
    velocity,
    land_mask,
    settling,
    breakage_rate,
    kernel_levels,
    pair_target,
    fragment_weights,
):
    local = (
        concentration,
        velocity,
        land_mask.reshape(COLS // 128, 128),
        settling.reshape(1, GROUP),
    )
    halves = f32(2, 2, GROUP, WIDTH)
    edge = f32(GROUP + 2, LAYERS, CY)
    inner, to_even, to_odd = call(
        inner_kernel,
        (halves, edge, edge),
        "inner",
        scratch=[pltpu.VMEM(x.shape, x.dtype) for x in local] + [pltpu.SemaphoreType.DMA((4,))],
        cost=1_000_000_000,
        in_specs=[pl.BlockSpec(memory_space=pltpu.HBM)] * 4,
    )(*[pltpu.with_memory_space_constraint(x, pltpu.HBM) for x in local])
    from_odd, from_even = swapped_in_pairs(to_odd, 1), swapped_in_pairs(to_even, 0)
    peer = swapped(inner[1], "near")
    tables = make_tables(kernel_levels, pair_target, fragment_weights, breakage_rate)
    outer, inner = call(outer_kernel, (halves, halves), "outer", cost=1_000_000_000)(
        *local, from_even, from_odd, inner, peer
    )
    inner_far = swapped(inner, "far")
    outer = jnp.concatenate([outer[:1], swapped(outer[1:], "near")], 0)
    outer_far = swapped(outer, "far")
    inner, inner_send = react(inner, inner_far, *tables, outer)
    outer, outer_send = react(outer, outer_far, *tables)
    inner_peer, outer_peer = swapped(inner_send, "near"), swapped(outer_send, "near")
    return call(lay_kernel, f32(GROUP, LAYERS, COLS), "lay")(inner, outer, inner_peer, outer_peer)


def solution(mesh):
    finer = Mesh(mesh.devices.reshape(mesh.shape["tile"], 2, 2), ("tile", "far", "near"))
    cls = ("far", "near")
    placed = (
        P(cls, None, "tile"),
        P(None, None, "tile"),
        P("tile"),
        P(cls),
        P(),
        P(),
        P(),
        P(),
    )
    return jax.shard_map(
        body, mesh=finer, in_specs=placed, out_specs=P(cls, None, "tile"), check_vma=False
    )
```

time: 72.7 us -> 61.4 us (0.84)
  the two profiles are of different devices: /device:TPU:215 before, /device:TPU:7 now
where the time goes in v2:
time: 61.4 us; the launch traced here: 61 us
  starting transfers between devices  29.4 us (48%)
  Pallas kernels  18.8 us (31%)
  waiting for transfers between devices  12.4 us (20%)
    ppermute x6, starting transfers between devices, swapped(): return lax.ppermute(x, axis, [(0, 1), (1, 0)])  21.8 us
    pallas_call x2, Pallas kernels, react(): call(react_kernel if len(arrays) == 5 else later_react_kernel, (half, hal...  14.9 us
    ppermute x6, waiting for transfers between devices, swapped(): return lax.ppermute(x, axis, [(0, 1), (1, 0)])  12.1 us
    ppermute x2, starting transfers between devices, swapped_in_pairs(): return lax.ppermute(x, 'tile', pairs + [(b, a) for a, b in pairs])  7.57 us
    pallas_call x1, Pallas kernels, body(): call(inner_kernel, (halves, edge, edge), 'inner', scratch=[pltpu.VMEM(x.s...  1.66 us
  transfers between devices with their start and end apart: 8, of which 5 were waited for; matrix products, arithmetic and copies ran while one was open for 0% of the time, Pallas kernels for 26%

profile of v2, /device:TPU:7, one launch (start us, length us, event | category | flops | bytes accessed | tf_op | source)
XLA Modules:
  0.0 61.0 jit_solution(12777082406331290588)
XLA Ops:
  0.0 1.7 %inner.1 = (f32[2,2,16,1024]{3,2,1,0:T(8,128)S(1)}, f32[18,4,512]{2,1,0:T(4,128)S(1)}, f32[18,4,512]{2,1,0:T(4,128)S(1)}) custom-call(f32[16,4,2048]{2,1,0:T(4,128)} %c_ref.1, f32[2,4,2048]{2,1,0:T(4,128)} %velocity_ref.1, s32[16,128]{1,0:T(8,128)} %bitcast.6, f32[1,16]{1,0:T(1,128)} %bitcast.8), custom_call_target="tpu_custom_call" | custom-call | flops 1000000000 | tf_op jit(solution)/shard_map/inner/pallas_call | solution.py:335
  1.7 3.2 %collective-permute-start = (f32[18,4,512]{2,1,0:T(4,128)S(1)}, f32[18,4,512]{2,1,0:T(4,128)S(1)}, u32[]{:S(2)}, u32[]{:S(2)}) collective-permute-start(f32[18,4,512]{2,1,0:T(4,128)S(1)} %get-tuple-element.17), channel_id=1, source_target_pairs={{0,4},{8,12},{16,20},{24,28},{32,36},{40,44},{48,52},{56,60},{64,6... | collective-permute-start | bytes 442376 | tf_op jit(solution)/shard_map/ppermute | solution.py:310
  4.9 4.4 %collective-permute-start.1 = (f32[18,4,512]{2,1,0:T(4,128)S(1)}, f32[18,4,512]{2,1,0:T(4,128)S(1)}, u32[]{:S(2)}, u32[]{:S(2)}) collective-permute-start(f32[18,4,512]{2,1,0:T(4,128)S(1)} %get-tuple-element.18), channel_id=1, source_target_pairs={{4,8},{12,16},{20,24},{28,32},{36,40},{44,48},{52,56},{60,64},{68,... | collective-permute-start | bytes 442376 | tf_op jit(solution)/shard_map/ppermute | solution.py:310
  9.3 0.0 copy-start
  9.3 0.0 copy-start.1
  9.3 0.0 copy-start.2
  9.3 0.0 copy-start.3
  9.3 3.3 %collective-permute-start.2 = (f32[2,16,1024]{2,1,0:T(8,128)S(1)}, f32[2,16,1024]{2,1,0:T(8,128)S(1)}, u32[]{:S(2)}, u32[]{:S(2)}) collective-permute-start(f32[2,16,1024]{2,1,0:T(8,128)S(1)} %slice_bitcast_fusion), channel_id=1, source_target_pairs={{0,1},{1,0},{2,3},{3,2},{4,5},{5,4},{6,7},{7,6},{8,9},{9,8},{10,11... | collective-permute-start | bytes 393224 | tf_op jit(solution)/shard_map/ppermute | solution.py:314
  12.6 1.0 %collective-permute-done.2.peer_ref = f32[2,16,1024]{2,1,0:T(8,128)S(1)} collective-permute-done((f32[2,16,1024]{2,1,0:T(8,128)S(1)}, f32[2,16,1024]{2,1,0:T(8,128)S(1)}, u32[]{:S(2)}, u32[]{:S(2)}) %collective-permute-start.2) | collective-permute-done | bytes 131104 | tf_op jit(solution)/shard_map/ppermute | solution.py:314
  13.6 0.0 collective-permute-done.even_ref
  13.6 0.4 collective-permute-done.1.odd_ref
  14.0 0.6 outer.1
  14.6 6.6 %collective-permute-start.3 = (f32[2,2,16,1024]{3,2,1,0:T(8,128)S(1)}, f32[2,2,16,1024]{3,2,1,0:T(8,128)S(1)}, u32[]{:S(2)}, u32[]{:S(2)}) collective-permute-start(f32[2,2,16,1024]{3,2,1,0:T(8,128)S(1)} %get-tuple-element.20.ours_ref), channel_id=1, source_target_pairs={{0,2},{2,0},{1,3},{3,1},{4,6},{6,4},{5,7},{7,5},{8,10},{10,8},{9,1... | collective-permute-start | bytes 786440 | tf_op jit(solution)/shard_map/ppermute | solution.py:314
  21.2 4.1 %collective-permute-start.4 = (f32[1,2,16,1024]{3,2,1,0:T(8,128)S(1)}, f32[1,2,16,1024]{3,2,1,0:T(8,128)S(1)}, u32[]{:S(2)}, u32[]{:S(2)}) collective-permute-start(f32[1,2,16,1024]{3,2,1,0:T(8,128)S(1)} %get-tuple-element.30), channel_id=1, source_target_pairs={{0,1},{1,0},{2,3},{3,2},{4,5},{5,4},{6,7},{7,6},{8,9},{9,8},{10,11... | collective-permute-start | bytes 393224 | tf_op jit(solution)/shard_map/ppermute | solution.py:314
  25.3 0.7 %tables.1 = (bf16[2304,256]{1,0:T(8,128)(2,1)S(1)}, bf16[1664,256]{1,0:T(8,128)(2,1)S(1)}, bf16[64,256]{1,0:T(8,128)(2,1)S(1)}) custom-call(s32[64,64]{1,0:T(8,128)S(1)} %copy-done, s32[64,64]{1,0:T(8,128)S(1)} %copy-done.1, s32[64,64]{1,0:T(8,128)S(1)} %copy-done.2, f32[1,64]{1,0:T(1,128)S(1)} %bitcast.5), custom_call_target="tpu_custom_call" | custom-call | tf_op jit(solution)/shard_map/tables/pallas_call | solution.py:94
  26.1 0.2 collective-permute-done.4
  26.3 2.6 %collective-permute-start.5 = (f32[2,2,16,1024]{3,2,1,0:T(8,128)S(1)}, f32[2,2,16,1024]{3,2,1,0:T(8,128)S(1)}, u32[]{:S(2)}, u32[]{:S(2)}) collective-permute-start(f32[2,2,16,1024]{3,2,1,0:T(8,128)S(1)} %pad_maximum_fusion._.ours_ref), channel_id=1, source_target_pairs={{0,2},{2,0},{1,3},{3,1},{4,6},{6,4},{5,7},{7,5},{8,10},{10,8},{9,1... | collective-permute-start | bytes 786440 | tf_op jit(solution)/shard_map/ppermute | solution.py:314
  28.9 7.5 %react.2 = (f32[2,16,1024]{2,1,0:T(8,128)S(1)}, f32[2,16,1024]{2,1,0:T(8,128)S(1)}) custom-call(f32[2,2,16,1024]{3,2,1,0:T(8,128)S(1)} %get-tuple-element.20.ours_ref, f32[2,2,16,1024]{3,2,1,0:T(8,128)S(1)} %collective-permute-done.3.theirs_ref, bf16[2304,256]{1,0:T(8,128)(2,1)S(1)} %get-tuple-element.21.all_ref, ...), custom_call_target="tpu_custom_call" | custom-call | flops 8000000000 | tf_op jit(solution)/shard_map/react/pallas_call | solution.py:286
  36.4 2.9 %collective-permute-start.6 = (f32[2,16,1024]{2,1,0:T(8,128)S(1)}, f32[2,16,1024]{2,1,0:T(8,128)S(1)}, u32[]{:S(2)}, u32[]{:S(2)}) collective-permute-start(f32[2,16,1024]{2,1,0:T(8,128)S(1)} %get-tuple-element.27), channel_id=1, source_target_pairs={{0,1},{1,0},{2,3},{3,2},{4,5},{5,4},{6,7},{7,6},{8,9},{9,8},{10,11... | collective-permute-start | bytes 393224 | tf_op jit(solution)/shard_map/ppermute | solution.py:314
  39.3 9.9 %collective-permute-done.5.theirs_ref = f32[2,2,16,1024]{3,2,1,0:T(8,128)S(1)} collective-permute-done((f32[2,2,16,1024]{3,2,1,0:T(8,128)S(1)}, f32[2,2,16,1024]{3,2,1,0:T(8,128)S(1)}, u32[]{:S(2)}, u32[]{:S(2)}) %collective-permute-start.5) | collective-permute-done | bytes 262176 | tf_op jit(solution)/shard_map/ppermute | solution.py:314
  49.3 7.4 %react.3 = (f32[2,16,1024]{2,1,0:T(8,128)S(1)}, f32[2,16,1024]{2,1,0:T(8,128)S(1)}) custom-call(f32[2,2,16,1024]{3,2,1,0:T(8,128)S(1)} %pad_maximum_fusion._.ours_ref, f32[2,2,16,1024]{3,2,1,0:T(8,128)S(1)} %collective-permute-done.5.theirs_ref, bf16[2304,256]{1,0:T(8,128)(2,1)S(1)} %get-tuple-element.21.all_ref, ...), custom_call_target="tpu_custom_call" | custom-call | flops 8000000000 | tf_op jit(solution)/shard_map/react/pallas_call | solution.py:286
  56.7 2.4 %collective-permute-start.7 = (f32[2,16,1024]{2,1,0:T(8,128)S(1)}, f32[2,16,1024]{2,1,0:T(8,128)S(1)}, u32[]{:S(2)}, u32[]{:S(2)}) collective-permute-start(f32[2,16,1024]{2,1,0:T(8,128)S(1)} %get-tuple-element.28), channel_id=1, source_target_pairs={{0,1},{1,0},{2,3},{3,2},{4,5},{5,4},{6,7},{7,6},{8,9},{9,8},{10,11... | collective-permute-start | bytes 393224 | tf_op jit(solution)/shard_map/ppermute | solution.py:314
  59.1 1.0 %collective-permute-done.7.outer_peer_ref = f32[2,16,1024]{2,1,0:T(8,128)S(1)} collective-permute-done((f32[2,16,1024]{2,1,0:T(8,128)S(1)}, f32[2,16,1024]{2,1,0:T(8,128)S(1)}, u32[]{:S(2)}, u32[]{:S(2)}) %collective-permute-start.7) | collective-permute-done | bytes 131104 | tf_op jit(solution)/shard_map/ppermute | solution.py:314
  60.1 0.9 %lay.1 = f32[16,4,2048]{2,1,0:T(4,128)} custom-call(f32[2,16,1024]{2,1,0:T(8,128)S(1)} %get-tuple-element.25.inner_ref, f32[2,16,1024]{2,1,0:T(8,128)S(1)} %get-tuple-element.26.outer_ref, f32[2,16,1024]{2,1,0:T(8,128)S(1)} %collective-permute-done.6.inner_peer_ref, f32[2,16,1024]{2,1,0:T(8,128)S(1)} %collective-permute-done.7.outer_peer_ref), custom_call_target="tpu_custom_call" | custom-call | tf_op jit(solution)/shard_map/lay/pallas_call | solution.py:355
  (17 shorter events, 0.1 us)
Async XLA Ops:
  0.0 14.0 %copy-start.4 = (f32[16,4,2048]{2,1,0:T(4,128)S(1)}, f32[16,4,2048]{2,1,0:T(4,128)}, u32[]{:S(2)}) copy-start(f32[16,4,2048]{2,1,0:T(4,128)} %c_ref.1) | copy-start | bytes 1572868
  0.0 14.0 %copy-start.5 = (f32[2,4,2048]{2,1,0:T(4,128)S(1)}, f32[2,4,2048]{2,1,0:T(4,128)}, u32[]{:S(2)}) copy-start(f32[2,4,2048]{2,1,0:T(4,128)} %velocity_ref.1) | copy-start | bytes 196612
  0.0 14.0 %copy-start.6 = (s32[2048]{0:T(1024)S(1)}, s32[2048]{0:T(1024)}, u32[]{:S(2)}) copy-start(s32[2048]{0:T(1024)} %param.10) | copy-start | bytes 24580
  0.0 14.0 %copy-start.7 = (f32[16]{0:T(128)S(1)}, f32[16]{0:T(128)}, u32[]{:S(2)}) copy-start(f32[16]{0:T(128)} %param.11) | copy-start | bytes 196
  1.7 11.9 %collective-permute-start = (f32[18,4,512]{2,1,0:T(4,128)S(1)}, f32[18,4,512]{2,1,0:T(4,128)S(1)}, u32[]{:S(2)}, u32[]{:S(2)}) collective-permute-start(f32[18,4,512]{2,1,0:T(4,128)S(1)} %get-tuple-element.17), channel_id=1, source_target_pairs={{0,4},{8,12},{16,20},{24,28},{32,36},{40,44},{48,52},{56,60},{64,6... | collective-permute-start | bytes 442376 | tf_op jit(solution)/shard_map/ppermute | solution.py:310
  4.9 9.1 %collective-permute-start.1 = (f32[18,4,512]{2,1,0:T(4,128)S(1)}, f32[18,4,512]{2,1,0:T(4,128)S(1)}, u32[]{:S(2)}, u32[]{:S(2)}) collective-permute-start(f32[18,4,512]{2,1,0:T(4,128)S(1)} %get-tuple-element.18), channel_id=1, source_target_pairs={{4,8},{12,16},{20,24},{28,32},{36,40},{44,48},{52,56},{60,64},{68,... | collective-permute-start | bytes 442376 | tf_op jit(solution)/shard_map/ppermute | solution.py:310
  9.3 16.0 %copy-start = (s32[64,64]{1,0:T(8,128)S(1)}, s32[64,64]{1,0:T(8,128)}, u32[]{:S(2)}) copy-start(s32[64,64]{1,0:T(8,128)} %levels_ref.1) | copy-start | bytes 49156
  9.3 16.0 %copy-start.1 = (s32[64,64]{1,0:T(8,128)S(1)}, s32[64,64]{1,0:T(8,128)}, u32[]{:S(2)}) copy-start(s32[64,64]{1,0:T(8,128)} %target_ref.1) | copy-start | bytes 49156
  9.3 16.0 %copy-start.2 = (s32[64,64]{1,0:T(8,128)S(1)}, s32[64,64]{1,0:T(8,128)}, u32[]{:S(2)}) copy-start(s32[64,64]{1,0:T(8,128)} %weights_ref.1) | copy-start | bytes 49156
  9.3 16.0 %copy-start.3 = (f32[64]{0:T(128)S(1)}, f32[64]{0:T(128)}, u32[]{:S(2)}) copy-start(f32[64]{0:T(128)} %param.12) | copy-start | bytes 772
  9.3 4.2 %collective-permute-start.2 = (f32[2,16,1024]{2,1,0:T(8,128)S(1)}, f32[2,16,1024]{2,1,0:T(8,128)S(1)}, u32[]{:S(2)}, u32[]{:S(2)}) collective-permute-start(f32[2,16,1024]{2,1,0:T(8,128)S(1)} %slice_bitcast_fusion), channel_id=1, source_target_pairs={{0,1},{1,0},{2,3},{3,2},{4,5},{5,4},{6,7},{7,6},{8,9},{9,8},{10,11... | collective-permute-start | bytes 393224 | tf_op jit(solution)/shard_map/ppermute | solution.py:314
  14.6 14.3 %collective-permute-start.3 = (f32[2,2,16,1024]{3,2,1,0:T(8,128)S(1)}, f32[2,2,16,1024]{3,2,1,0:T(8,128)S(1)}, u32[]{:S(2)}, u32[]{:S(2)}) collective-permute-start(f32[2,2,16,1024]{3,2,1,0:T(8,128)S(1)} %get-tuple-element.20.ours_ref), channel_id=1, source_target_pairs={{0,2},{2,0},{1,3},{3,1},{4,6},{6,4},{5,7},{7,5},{8,10},{10,8},{9,1... | collective-permute-start | bytes 786440 | tf_op jit(solution)/shard_map/ppermute | solution.py:314
  21.2 5.0 %collective-permute-start.4 = (f32[1,2,16,1024]{3,2,1,0:T(8,128)S(1)}, f32[1,2,16,1024]{3,2,1,0:T(8,128)S(1)}, u32[]{:S(2)}, u32[]{:S(2)}) collective-permute-start(f32[1,2,16,1024]{3,2,1,0:T(8,128)S(1)} %get-tuple-element.30), channel_id=1, source_target_pairs={{0,1},{1,0},{2,3},{3,2},{4,5},{5,4},{6,7},{7,6},{8,9},{9,8},{10,11... | collective-permute-start | bytes 393224 | tf_op jit(solution)/shard_map/ppermute | solution.py:314
  26.3 23.0 %collective-permute-start.5 = (f32[2,2,16,1024]{3,2,1,0:T(8,128)S(1)}, f32[2,2,16,1024]{3,2,1,0:T(8,128)S(1)}, u32[]{:S(2)}, u32[]{:S(2)}) collective-permute-start(f32[2,2,16,1024]{3,2,1,0:T(8,128)S(1)} %pad_maximum_fusion._.ours_ref), channel_id=1, source_target_pairs={{0,2},{2,0},{1,3},{3,1},{4,6},{6,4},{5,7},{7,5},{8,10},{10,8},{9,1... | collective-permute-start | bytes 786440 | tf_op jit(solution)/shard_map/ppermute | solution.py:314
  36.4 22.7 %collective-permute-start.6 = (f32[2,16,1024]{2,1,0:T(8,128)S(1)}, f32[2,16,1024]{2,1,0:T(8,128)S(1)}, u32[]{:S(2)}, u32[]{:S(2)}) collective-permute-start(f32[2,16,1024]{2,1,0:T(8,128)S(1)} %get-tuple-element.27), channel_id=1, source_target_pairs={{0,1},{1,0},{2,3},{3,2},{4,5},{5,4},{6,7},{7,6},{8,9},{9,8},{10,11... | collective-permute-start | bytes 393224 | tf_op jit(solution)/shard_map/ppermute | solution.py:314
  56.7 3.3 %collective-permute-start.7 = (f32[2,16,1024]{2,1,0:T(8,128)S(1)}, f32[2,16,1024]{2,1,0:T(8,128)S(1)}, u32[]{:S(2)}, u32[]{:S(2)}) collective-permute-start(f32[2,16,1024]{2,1,0:T(8,128)S(1)} %get-tuple-element.28), channel_id=1, source_target_pairs={{0,1},{1,0},{2,3},{3,2},{4,5},{5,4},{6,7},{7,6},{8,9},{9,8},{10,11... | collective-permute-start | bytes 393224 | tf_op jit(solution)/shard_map/ppermute | solution.py:314

commit v3 on v2

--- a/solution.py
+++ b/solution.py
@@ -13,7 +13,9 @@
 GROUP = 16
 COLS = CX * CY
 WIDTH = 2 * CY
-TILE = 256
+TILE = 512
+LANES = 4
+DOTS = [[0, 1], [2, 3], [4, 5, 6, 7]]
 HALF_SCALE = 0.5e-05
 VMEM_LIMIT = 48 * 1024 * 1024
 
@@ -148,31 +150,35 @@
         out_ref[(near + layer // 2) % 2, layer % 2] = moved
 
 
-def inner_kernel(*refs):
-    taken, made = refs[:4], refs[4:7]
-    here, sems = refs[7:11], refs[11]
-    copies = [
-        pltpu.make_async_copy(src, dst, sems.at[k]) for k, (src, dst) in enumerate(zip(taken, here))
-    ]
+def fetched(pairs, sems):
+    copies = [pltpu.make_async_copy(*pair, sems.at[k]) for k, pair in enumerate(pairs)]
     for copy in copies:
         copy.start()
     for copy in copies:
         copy.wait()
-    inner_rows(*here, *made)
-
-
-def inner_rows(c_ref, velocity_ref, mask_ref, settling_ref, out_ref, *edge_refs):
+
+
+def edge_kernel(c_ref, velocity_ref, mask_ref, to_even_ref, to_odd_ref, mask, u, sems):
+    even = lax.axis_index("tile") % 2
+    ends = [pl.ds(pl.multiple_of(at * (COLS - CY), CY), CY) for at in (1 - even, even)]
+    outs = (to_even_ref, to_odd_ref)
+    pairs = [(mask_ref, mask), (velocity_ref.at[0], u)]
+    pairs += [(c_ref.at[:, :, end], out.at[:GROUP]) for end, out in zip(ends, outs)]
+    fetched(pairs, sems)
+    water = water_of(mask)
+    for out, last in zip(outs, (even == 0, even != 0)):
+        out[GROUP] = jnp.where(last, u[:, COLS - CY :], u[:, :CY])
+        w = jnp.where(last, water[:, COLS - CY :], water[:, :CY])
+        out[GROUP + 1] = jnp.broadcast_to(w, (LAYERS, CY))
+
+
+def inner_kernel(*refs):
+    fetched(zip(refs[:4], refs[5:9]), refs[9])
+    inner_rows(*refs[5:9], refs[4])
+
+
+def inner_rows(c_ref, velocity_ref, mask_ref, settling_ref, out_ref):
     water = water_of(mask_ref)
-    even = lax.axis_index("tile") % 2 == 0
-
-    def rows(x):
-        first, last = x[..., :CY], x[..., COLS - CY :]
-        return jnp.where(even, last, first), jnp.where(even, first, last)
-
-    for ref, c, u, w in zip(edge_refs, rows(c_ref[...]), rows(velocity_ref[0]), rows(water)):
-        ref[:GROUP] = c
-        ref[GROUP] = u
-        ref[GROUP + 1] = jnp.broadcast_to(w, (LAYERS, CY))
 
     def three(x):
         return x[:, : 2 * CY], x[:, CY : 3 * CY], x[:, 2 * CY :]
@@ -231,17 +237,19 @@
 
 def gains(n, stack, table_ref, spans, first, count):
     total = [jnp.zeros((8, TILE), jnp.float32) for _ in range(count // 8)]
-    for b in range(BLOCKS):
-        span = spans[b]
+    for blocks in DOTS:
+        base = first[blocks[0]]
         made = jnp.dot(
-            table_ref[first[b] : first[b + 1], :], stack, preferred_element_type=jnp.float32
+            table_ref[base : first[blocks[-1] + 1], :], stack, preferred_element_type=jnp.float32
         )
-        skip = (count - span) // 8
-        for ii in range(8):
-            partner = n[8 * b + ii : 8 * b + ii + 1]
-            for g in range(span // 8):
-                row = ii * span + 8 * g
-                total[skip + g] = total[skip + g] + made[row : row + 8] * partner
+        for b in blocks:
+            span = spans[b]
+            skip = (count - span) // 8
+            for ii in range(8):
+                partner = n[8 * b + ii : 8 * b + ii + 1]
+                for g in range(span // 8):
+                    row = first[b] - base + ii * span + 8 * g
+                    total[skip + g] = total[skip + g] + made[row : row + 8] * partner
     return jnp.concatenate(total, 0)
 
 
@@ -250,57 +258,73 @@
     return jnp.concatenate([high, low, high, low], 0)
 
 
-def later_react_kernel(ours_ref, theirs_ref, all_ref, own_ref, linear_ref, _, *rest):
-    react_kernel(ours_ref, theirs_ref, all_ref, own_ref, linear_ref, *rest)
-
-
-def react_kernel(ours_ref, theirs_ref, all_ref, own_ref, linear_ref, keep_ref, send_ref, whole):
+def react_kernel(ours_ref, theirs_ref, all_ref, own_ref, linear_ref, *rest):
+    keep_ref, send_ref, whole = rest[-3:]
+    lanes = whole.shape[0]
+    layers = ours_ref.shape[1]
+    filled = 0
+    if send_ref.shape[0] > layers:
+        for ref in rest[:-3]:
+            send_ref[filled : filled + ref.shape[0]] = ref[...]
+            filled += ref.shape[0]
     far, near = lax.axis_index("far"), lax.axis_index("near")
     groups = [2 * f + n for f in (far, 1 - far) for n in (near, 1 - near)]
     parts = [ref.at[place] for ref in (ours_ref, theirs_ref) for place in range(2)]
 
-    def tile(index, carry):
-        slot = index // (WIDTH // TILE)
-        at = pl.ds(pl.multiple_of((index % (WIDTH // TILE)) * TILE, TILE), TILE)
-        for group, part in zip(groups, parts):
-            whole[group] = part[slot, :, at]
-        n = whole[...].reshape(NC, TILE)
-        stack = stack_of(n)
-        made = gains(n, stack, all_ref, ALL_SPANS, ALL_STARTS, NC)
-        linear = jnp.dot(linear_ref[...], stack, preferred_element_type=jnp.float32)
-        n = n + (HALF_SCALE * made + linear)
-        stack = stack_of(n)
-        made = gains(n, stack, own_ref, OWN_SPANS, OWN_STARTS, NC // 2)
+    def step(index, carry):
+        places = []
+        for k in range(lanes):
+            at = index * lanes + k
+            slot = at // (WIDTH // TILE)
+            places.append((slot, pl.ds(pl.multiple_of((at % (WIDTH // TILE)) * TILE, TILE), TILE)))
+        ns = []
+        for k, (slot, at) in enumerate(places):
+            for group, part in zip(groups, parts):
+                whole[k, group] = part[slot, :, at]
+            ns.append(whole[k].reshape(NC, TILE))
+        stacks = [stack_of(n) for n in ns]
+        mades = [gains(*both, all_ref, ALL_SPANS, ALL_STARTS, NC) for both in zip(ns, stacks)]
+        linears = [
+            jnp.dot(linear_ref[...], stack, preferred_element_type=jnp.float32) for stack in stacks
+        ]
+        ns = [n + (HALF_SCALE * made + linear) for n, made, linear in zip(ns, mades, linears)]
+        stacks = [stack_of(n) for n in ns]
+        mades = [gains(*both, own_ref, OWN_SPANS, OWN_STARTS, NC // 2) for both in zip(ns, stacks)]
         mine = linear_ref[pl.ds(pl.multiple_of(far * (NC // 2), NC // 2), NC // 2), :]
-        linear = jnp.dot(mine, stack, preferred_element_type=jnp.float32)
-        n = jnp.where(far == 0, n[: NC // 2], n[NC // 2 :]) + (HALF_SCALE * made + linear)
-        keep_ref[slot, :, at] = jnp.where(near == 0, n[:GROUP], n[GROUP:])
-        send_ref[slot, :, at] = jnp.where(near == 0, n[GROUP:], n[:GROUP])
+        linears = [
+            jnp.dot(mine, stack, preferred_element_type=jnp.float32) for stack in stacks
+        ]
+        for n, made, linear, (slot, at) in zip(ns, mades, linears, places):
+            n = jnp.where(far == 0, n[: NC // 2], n[NC // 2 :]) + (HALF_SCALE * made + linear)
+            keep_ref[slot, :, at] = jnp.where(near == 0, n[:GROUP], n[GROUP:])
+            send_ref[filled + slot, :, at] = jnp.where(near == 0, n[GROUP:], n[:GROUP])
         return carry
 
-    lax.fori_loop(0, 2 * WIDTH // TILE, tile, 0)
-
-
-def react(*arrays):
-    half = f32(2, GROUP, WIDTH)
+    lax.fori_loop(0, layers * WIDTH // (lanes * TILE), step, 0)
+
+
+def react(ours, theirs, tables, later=(), earlier=()):
+    layers = ours.shape[1]
+    sent = layers + sum(x.shape[0] for x in earlier)
     return call(
-        react_kernel if len(arrays) == 5 else later_react_kernel,
-        (half, half),
+        react_kernel,
+        (f32(layers, GROUP, WIDTH), f32(sent, GROUP, WIDTH)),
         "react",
-        scratch=[pltpu.VMEM((4, GROUP, TILE), jnp.float32)],
-        cost=8_000_000_000,
-        in_specs=[pl.BlockSpec(memory_space=pltpu.VMEM)] * 5
-        + [pl.BlockSpec(memory_space=pl.ANY)] * (len(arrays) - 5),
-    )(*arrays)
-
-
-def lay_kernel(inner_ref, outer_ref, inner_peer_ref, outer_peer_ref, out_ref):
+        scratch=[pltpu.VMEM((min(LANES, layers * WIDTH // TILE), 4, GROUP, TILE), jnp.float32)],
+        cost=3_000_000_000 * layers,
+        in_specs=[pl.BlockSpec(memory_space=pltpu.VMEM)] * (5 + len(earlier))
+        + [pl.BlockSpec(memory_space=pl.ANY)] * len(later),
+    )(ours, theirs, *tables, *earlier, *later)
+
+
+def lay_kernel(inner_ref, first_ref, second_ref, peer_ref, out_ref):
     near = lax.axis_index("near")
+    outer_refs = (first_ref, second_ref)
     for layer in range(LAYERS):
         slot = layer % 2
         mine = near == layer // 2
-        inner = jnp.where(mine, inner_ref[slot], inner_peer_ref[slot])
-        outer = jnp.where(mine, outer_ref[slot], outer_peer_ref[slot])
+        inner = jnp.where(mine, inner_ref[slot], peer_ref[slot])
+        outer = jnp.where(mine, outer_refs[slot][0], peer_ref[2 + slot])
         out_ref[:, layer, :] = jnp.concatenate([outer[:, :CY], inner, outer[:, CY:]], 1)
 
 
@@ -332,27 +356,40 @@
     )
     halves = f32(2, 2, GROUP, WIDTH)
     edge = f32(GROUP + 2, LAYERS, CY)
-    inner, to_even, to_odd = call(
+    placed = [pltpu.with_memory_space_constraint(x, pltpu.HBM) for x in local]
+    to_even, to_odd = call(
+        edge_kernel,
+        (edge, edge),
+        "edges",
+        scratch=[
+            pltpu.VMEM(local[2].shape, jnp.int32),
+            pltpu.VMEM((LAYERS, COLS), jnp.float32),
+            pltpu.SemaphoreType.DMA((4,)),
+        ],
+        in_specs=[pl.BlockSpec(memory_space=pltpu.HBM)] * 3,
+    )(*placed[:3])
+    from_odd, from_even = swapped_in_pairs(to_odd, 1), swapped_in_pairs(to_even, 0)
+    inner = call(
         inner_kernel,
-        (halves, edge, edge),
+        halves,
         "inner",
         scratch=[pltpu.VMEM(x.shape, x.dtype) for x in local] + [pltpu.SemaphoreType.DMA((4,))],
-        cost=1_000_000_000,
         in_specs=[pl.BlockSpec(memory_space=pltpu.HBM)] * 4,
-    )(*[pltpu.with_memory_space_constraint(x, pltpu.HBM) for x in local])
-    from_odd, from_even = swapped_in_pairs(to_odd, 1), swapped_in_pairs(to_even, 0)
+    )(*placed)
     peer = swapped(inner[1], "near")
     tables = make_tables(kernel_levels, pair_target, fragment_weights, breakage_rate)
     outer, inner = call(outer_kernel, (halves, halves), "outer", cost=1_000_000_000)(
         *local, from_even, from_odd, inner, peer
     )
     inner_far = swapped(inner, "far")
-    outer = jnp.concatenate([outer[:1], swapped(outer[1:], "near")], 0)
-    outer_far = swapped(outer, "far")
-    inner, inner_send = react(inner, inner_far, *tables, outer)
-    outer, outer_send = react(outer, outer_far, *tables)
-    inner_peer, outer_peer = swapped(inner_send, "near"), swapped(outer_send, "near")
-    return call(lay_kernel, f32(GROUP, LAYERS, COLS), "lay")(inner, outer, inner_peer, outer_peer)
+    outer_peer = swapped(outer[1:], "near")
+    ours = [jnp.concatenate([outer[:1, k : k + 1], outer_peer[:, k : k + 1]], 0) for k in range(2)]
+    theirs = [swapped(x, "far") for x in ours]
+    inner, sent = react(inner, inner_far, tables, later=ours)
+    first, sent_first = react(ours[0], theirs[0], tables)
+    second, sent = react(ours[1], theirs[1], tables, earlier=(sent, sent_first))
+    peer = swapped(sent, "near")
+    return call(lay_kernel, f32(GROUP, LAYERS, COLS), "lay")(inner, first, second, peer)
 
 
 def solution(mesh):

time: 61.4 us -> 56.2 us (0.915)
  waiting for transfers between devices: 12.4 us -> 8.22 us
  Pallas kernels: 18.8 us -> 14.9 us
  starting transfers between devices: 29.4 us -> 32.3 us
    pallas_call x3 -> x5, Pallas kernels: 16.6 us -> 12.7 us  [the longest x3 9.99 us: react(): call(react_kernel, (f32(layers, GROUP, WIDTH), f32(sent, GROUP, WIDTH)),...]
    ppermute x6, waiting for transfers between devices: 12.1 us -> 8.22 us  [swapped(): return lax.ppermute(x, axis, [(0, 1), (1, 0)])]
    ppermute x6, starting transfers between devices: 21.8 us -> 24.7 us  [swapped(): return lax.ppermute(x, axis, [(0, 1), (1, 0)])]
  transfers between devices with their start and end apart: 8 -> 8, of which waited for: 5 -> 5; matrix products, arithmetic and copies ran while one was open for 0% -> 0% of each run, Pallas kernels for 26% -> 17%
where the time goes in v3:
time: 56.2 us; the launch traced here: 55.8 us
  starting transfers between devices  32.3 us (57%)
  Pallas kernels  14.9 us (27%)
  waiting for transfers between devices  8.22 us (15%)
    ppermute x6, starting transfers between devices, swapped(): return lax.ppermute(x, axis, [(0, 1), (1, 0)])  24.7 us
    pallas_call x3, Pallas kernels, react(): call(react_kernel, (f32(layers, GROUP, WIDTH), f32(sent, GROUP, WIDTH)),...  9.99 us
    ppermute x6, waiting for transfers between devices, swapped(): return lax.ppermute(x, axis, [(0, 1), (1, 0)])  8.22 us
    ppermute x2, starting transfers between devices, swapped_in_pairs(): return lax.ppermute(x, 'tile', pairs + [(b, a) for a, b in pairs])  7.57 us
    pallas_call x1, Pallas kernels, body(): call(inner_kernel, halves, 'inner', scratch=[pltpu.VMEM(x.shape, x.dtype)...  1.59 us
  transfers between devices with their start and end apart: 8, of which 5 were waited for; matrix products, arithmetic and copies ran while one was open for 0% of the time, Pallas kernels for 17%

profile of v3, /device:TPU:7, one launch (start us, length us, event | category | flops | bytes accessed | tf_op | source)
XLA Modules:
  0.0 55.8 jit_solution(7307019424067166275)
XLA Ops:
  0.0 0.0 copy-start.7
  0.1 1.1 %edges.1 = (f32[18,4,512]{2,1,0:T(4,128)S(1)}, f32[18,4,512]{2,1,0:T(4,128)S(1)}) custom-call(f32[16,4,2048]{2,1,0:T(4,128)} %c_ref.3, f32[2,4,2048]{2,1,0:T(4,128)} %velocity_ref.3, s32[16,128]{1,0:T(8,128)} %bitcast.5), custom_call_target="tpu_custom_call" | custom-call | tf_op jit(solution)/shard_map/edges/pallas_call | solution.py:360
  1.2 3.2 %collective-permute-start = (f32[18,4,512]{2,1,0:T(4,128)S(1)}, f32[18,4,512]{2,1,0:T(4,128)S(1)}, u32[]{:S(2)}, u32[]{:S(2)}) collective-permute-start(f32[18,4,512]{2,1,0:T(4,128)S(1)} %get-tuple-element.18), channel_id=1, source_target_pairs={{0,4},{8,12},{16,20},{24,28},{32,36},{40,44},{48,52},{56,60},{64,6... | collective-permute-start | bytes 442376 | tf_op jit(solution)/shard_map/ppermute | solution.py:334
  4.4 4.4 %collective-permute-start.1 = (f32[18,4,512]{2,1,0:T(4,128)S(1)}, f32[18,4,512]{2,1,0:T(4,128)S(1)}, u32[]{:S(2)}, u32[]{:S(2)}) collective-permute-start(f32[18,4,512]{2,1,0:T(4,128)S(1)} %get-tuple-element.19), channel_id=1, source_target_pairs={{4,8},{12,16},{20,24},{28,32},{36,40},{44,48},{52,56},{60,64},{68,... | collective-permute-start | bytes 442376 | tf_op jit(solution)/shard_map/ppermute | solution.py:334
  8.8 1.6 %inner.1.inner_ref = f32[2,2,16,1024]{3,2,1,0:T(8,128)S(1)} custom-call(f32[16,4,2048]{2,1,0:T(4,128)} %c_ref.3, f32[2,4,2048]{2,1,0:T(4,128)} %velocity_ref.3, s32[16,128]{1,0:T(8,128)} %bitcast.6, f32[1,16]{1,0:T(1,128)} %bitcast.9), custom_call_target="tpu_custom_call" | custom-call | tf_op jit(solution)/shard_map/inner/pallas_call | solution.py:372
  10.4 3.1 %collective-permute-start.2 = (f32[2,16,1024]{2,1,0:T(8,128)S(1)}, f32[2,16,1024]{2,1,0:T(8,128)S(1)}, u32[]{:S(2)}, u32[]{:S(2)}) collective-permute-start(f32[2,16,1024]{2,1,0:T(8,128)S(1)} %slice_bitcast_fusion), channel_id=1, source_target_pairs={{0,1},{1,0},{2,3},{3,2},{4,5},{5,4},{6,7},{7,6},{8,9},{9,8},{10,11... | collective-permute-start | bytes 393224 | tf_op jit(solution)/shard_map/ppermute | solution.py:338
  13.6 0.7 %tables.1 = (bf16[2304,256]{1,0:T(8,128)(2,1)S(1)}, bf16[1664,256]{1,0:T(8,128)(2,1)S(1)}, bf16[64,256]{1,0:T(8,128)(2,1)S(1)}) custom-call(s32[64,64]{1,0:T(8,128)S(1)} %copy-done.3, s32[64,64]{1,0:T(8,128)S(1)} %copy-done.4, s32[64,64]{1,0:T(8,128)S(1)} %copy-done.5, f32[1,64]{1,0:T(1,128)S(1)} %bitcast.8), custom_call_target="tpu_custom_call" | custom-call | tf_op jit(solution)/shard_map/tables/pallas_call | solution.py:96
  14.3 0.2 collective-permute-done.2.peer_ref
  14.5 0.0 collective-permute-done.even_ref
  14.5 0.6 %outer.1 = (f32[2,2,16,1024]{3,2,1,0:T(8,128)S(1)}, f32[2,2,16,1024]{3,2,1,0:T(8,128)S(1)}) custom-call(f32[16,4,2048]{2,1,0:T(4,128)S(1)} %copy-done, f32[2,4,2048]{2,1,0:T(4,128)S(1)} %copy-done.1, s32[16,128]{1,0:T(8,128)S(1)} %bitcast.7, f32[1,16]{1,0:T(1,128)S(1)} %bitcast.10, f32[18,4,512]{2,1,0:T(4,128)S(1)} %collective-permute-done.even_ref, ...), custom_call_target="tpu_custom_call" | custom-call | flops 1000000000 | tf_op jit(solution)/shard_map/outer/pallas_call | solution.py:381
  15.2 5.7 %collective-permute-start.3 = (f32[2,2,16,1024]{3,2,1,0:T(8,128)S(1)}, f32[2,2,16,1024]{3,2,1,0:T(8,128)S(1)}, u32[]{:S(2)}, u32[]{:S(2)}) collective-permute-start(f32[2,2,16,1024]{3,2,1,0:T(8,128)S(1)} %get-tuple-element.20.ours_ref), channel_id=1, source_target_pairs={{0,2},{2,0},{1,3},{3,1},{4,6},{6,4},{5,7},{7,5},{8,10},{10,8},{9,1... | collective-permute-start | bytes 786440 | tf_op jit(solution)/shard_map/ppermute | solution.py:338
  20.8 3.9 %collective-permute-start.4 = (f32[1,2,16,1024]{3,2,1,0:T(8,128)S(1)}, f32[1,2,16,1024]{3,2,1,0:T(8,128)S(1)}, u32[]{:S(2)}, u32[]{:S(2)}) collective-permute-start(f32[1,2,16,1024]{3,2,1,0:T(8,128)S(1)} %slice.20), channel_id=1, source_target_pairs={{0,1},{1,0},{2,3},{3,2},{4,5},{5,4},{6,7},{7,6},{8,9},{9,8},{10,11... | collective-permute-start | bytes 393224 | tf_op jit(solution)/shard_map/ppermute | solution.py:338
  24.8 0.9 %collective-permute-done.4 = f32[1,2,16,1024]{3,2,1,0:T(8,128)S(1)} collective-permute-done((f32[1,2,16,1024]{3,2,1,0:T(8,128)S(1)}, f32[1,2,16,1024]{3,2,1,0:T(8,128)S(1)}, u32[]{:S(2)}, u32[]{:S(2)}) %collective-permute-start.4) | collective-permute-done | bytes 131104 | tf_op jit(solution)/shard_map/ppermute | solution.py:338
  25.8 2.6 %collective-permute-start.5 = (f32[2,1,16,1024]{3,2,1,0:T(8,128)S(1)}, f32[2,1,16,1024]{3,2,1,0:T(8,128)S(1)}, u32[]{:S(2)}, u32[]{:S(2)}) collective-permute-start(f32[2,1,16,1024]{3,2,1,0:T(8,128)S(1)} %pad_maximum_fusion.rest_0_.ours_ref), channel_id=1, source_target_pairs={{0,2},{2,0},{1,3},{3,1},{4,6},{6,4},{5,7},{7,5},{8,10},{10,8},{9,1... | collective-permute-start | bytes 393224 | tf_op jit(solution)/shard_map/ppermute | solution.py:338
  28.4 6.7 %collective-permute-start.6 = (f32[2,1,16,1024]{3,2,1,0:T(8,128)S(1)}, f32[2,1,16,1024]{3,2,1,0:T(8,128)S(1)}, u32[]{:S(2)}, u32[]{:S(2)}) collective-permute-start(f32[2,1,16,1024]{3,2,1,0:T(8,128)S(1)} %pad_maximum_fusion.1.rest_1_.ours_ref), channel_id=1, source_target_pairs={{0,2},{2,0},{1,3},{3,1},{4,6},{6,4},{5,7},{7,5},{8,10},{10,8},{9,1... | collective-permute-start | bytes 393224 | tf_op jit(solution)/shard_map/ppermute | solution.py:338
  35.2 0.0 collective-permute-done.3.theirs_ref
  35.2 4.9 %react.3 = (f32[2,16,1024]{2,1,0:T(8,128)S(1)}, f32[2,16,1024]{2,1,0:T(8,128)S(1)}) custom-call(f32[2,2,16,1024]{3,2,1,0:T(8,128)S(1)} %get-tuple-element.20.ours_ref, f32[2,2,16,1024]{3,2,1,0:T(8,128)S(1)} %collective-permute-done.3.theirs_ref, bf16[2304,256]{1,0:T(8,128)(2,1)S(1)} %get-tuple-element.21.all_ref, ...), custom_call_target="tpu_custom_call" | custom-call | flops 6000000000 | tf_op jit(solution)/shard_map/react/pallas_call | solution.py:309
  40.1 5.7 %collective-permute-done.5.theirs_ref = f32[2,1,16,1024]{3,2,1,0:T(8,128)S(1)} collective-permute-done((f32[2,1,16,1024]{3,2,1,0:T(8,128)S(1)}, f32[2,1,16,1024]{3,2,1,0:T(8,128)S(1)}, u32[]{:S(2)}, u32[]{:S(2)}) %collective-permute-start.5) | collective-permute-done | bytes 131104 | tf_op jit(solution)/shard_map/ppermute | solution.py:338
  45.8 2.6 %react.4 = (f32[1,16,1024]{2,1,0:T(8,128)S(1)}, f32[1,16,1024]{2,1,0:T(8,128)S(1)}) custom-call(f32[2,1,16,1024]{3,2,1,0:T(8,128)S(1)} %pad_maximum_fusion.rest_0_.ours_ref, f32[2,1,16,1024]{3,2,1,0:T(8,128)S(1)} %collective-permute-done.5.theirs_ref, bf16[2304,256]{1,0:T(8,128)(2,1)S(1)} %get-tuple-element.21.all_ref, ...), custom_call_target="tpu_custom_call" | custom-call | flops 3000000000 | tf_op jit(solution)/shard_map/react/pallas_call | solution.py:309
  48.3 0.2 collective-permute-done.6.theirs_ref
  48.6 2.6 %react.5 = (f32[1,16,1024]{2,1,0:T(8,128)S(1)}, f32[4,16,1024]{2,1,0:T(8,128)S(1)}) custom-call(f32[2,1,16,1024]{3,2,1,0:T(8,128)S(1)} %pad_maximum_fusion.1.rest_1_.ours_ref, f32[2,1,16,1024]{3,2,1,0:T(8,128)S(1)} %collective-permute-done.6.theirs_ref, bf16[2304,256]{1,0:T(8,128)(2,1)S(1)} %get-tuple-element.21.all_ref, ...), custom_call_target="tpu_custom_call" | custom-call | flops 3000000000 | tf_op jit(solution)/shard_map/react/pallas_call | solution.py:309
  51.1 2.6 %collective-permute-start.7 = (f32[4,16,1024]{2,1,0:T(8,128)S(1)}, f32[4,16,1024]{2,1,0:T(8,128)S(1)}, u32[]{:S(2)}, u32[]{:S(2)}) collective-permute-start(f32[4,16,1024]{2,1,0:T(8,128)S(1)} %get-tuple-element.30), channel_id=1, source_target_pairs={{0,1},{1,0},{2,3},{3,2},{4,5},{5,4},{6,7},{7,6},{8,9},{9,8},{10,11... | collective-permute-start | bytes 786440 | tf_op jit(solution)/shard_map/ppermute | solution.py:338
  53.8 1.1 %collective-permute-done.7.peer_ref = f32[4,16,1024]{2,1,0:T(8,128)S(1)} collective-permute-done((f32[4,16,1024]{2,1,0:T(8,128)S(1)}, f32[4,16,1024]{2,1,0:T(8,128)S(1)}, u32[]{:S(2)}, u32[]{:S(2)}) %collective-permute-start.7) | collective-permute-done | bytes 262176 | tf_op jit(solution)/shard_map/ppermute | solution.py:338
  54.9 0.9 %lay.1 = f32[16,4,2048]{2,1,0:T(4,128)} custom-call(f32[2,16,1024]{2,1,0:T(8,128)S(1)} %get-tuple-element.25.inner_ref, f32[1,16,1024]{2,1,0:T(8,128)S(1)} %get-tuple-element.26.first_ref, f32[1,16,1024]{2,1,0:T(8,128)S(1)} %get-tuple-element.29.second_ref, f32[4,16,1024]{2,1,0:T(8,128)S(1)} %collective-permute-done.7.peer_ref), custom_call_target="tpu_custom_call" | custom-call | tf_op jit(solution)/shard_map/lay/pallas_call | solution.py:392
  (22 shorter events, 0.1 us)
Async XLA Ops:
  0.0 14.5 %copy-start = (f32[16,4,2048]{2,1,0:T(4,128)S(1)}, f32[16,4,2048]{2,1,0:T(4,128)}, u32[]{:S(2)}) copy-start(f32[16,4,2048]{2,1,0:T(4,128)} %c_ref.3) | copy-start | bytes 1572868
  0.0 14.5 %copy-start.1 = (f32[2,4,2048]{2,1,0:T(4,128)S(1)}, f32[2,4,2048]{2,1,0:T(4,128)}, u32[]{:S(2)}) copy-start(f32[2,4,2048]{2,1,0:T(4,128)} %velocity_ref.3) | copy-start | bytes 196612
  0.0 14.5 %copy-start.2 = (s32[2048]{0:T(1024)S(1)}, s32[2048]{0:T(1024)}, u32[]{:S(2)}) copy-start(s32[2048]{0:T(1024)} %param.10) | copy-start | bytes 24580
  0.0 14.5 %copy-start.7 = (f32[16]{0:T(128)S(1)}, f32[16]{0:T(128)}, u32[]{:S(2)}) copy-start(f32[16]{0:T(128)} %param.11) | copy-start | bytes 196
  0.0 13.5 %copy-start.3 = (s32[64,64]{1,0:T(8,128)S(1)}, s32[64,64]{1,0:T(8,128)}, u32[]{:S(2)}) copy-start(s32[64,64]{1,0:T(8,128)} %levels_ref.1) | copy-start | bytes 49156
  0.0 13.5 %copy-start.4 = (s32[64,64]{1,0:T(8,128)S(1)}, s32[64,64]{1,0:T(8,128)}, u32[]{:S(2)}) copy-start(s32[64,64]{1,0:T(8,128)} %target_ref.1) | copy-start | bytes 49156
  0.0 13.5 %copy-start.5 = (s32[64,64]{1,0:T(8,128)S(1)}, s32[64,64]{1,0:T(8,128)}, u32[]{:S(2)}) copy-start(s32[64,64]{1,0:T(8,128)} %weights_ref.1) | copy-start | bytes 49156
  0.1 13.5 %copy-start.6 = (f32[64]{0:T(128)S(1)}, f32[64]{0:T(128)}, u32[]{:S(2)}) copy-start(f32[64]{0:T(128)} %param.12) | copy-start | bytes 772
  1.2 13.3 %collective-permute-start = (f32[18,4,512]{2,1,0:T(4,128)S(1)}, f32[18,4,512]{2,1,0:T(4,128)S(1)}, u32[]{:S(2)}, u32[]{:S(2)}) collective-permute-start(f32[18,4,512]{2,1,0:T(4,128)S(1)} %get-tuple-element.18), channel_id=1, source_target_pairs={{0,4},{8,12},{16,20},{24,28},{32,36},{40,44},{48,52},{56,60},{64,6... | collective-permute-start | bytes 442376 | tf_op jit(solution)/shard_map/ppermute | solution.py:334
  4.4 10.1 %collective-permute-start.1 = (f32[18,4,512]{2,1,0:T(4,128)S(1)}, f32[18,4,512]{2,1,0:T(4,128)S(1)}, u32[]{:S(2)}, u32[]{:S(2)}) collective-permute-start(f32[18,4,512]{2,1,0:T(4,128)S(1)} %get-tuple-element.19), channel_id=1, source_target_pairs={{4,8},{12,16},{20,24},{28,32},{36,40},{44,48},{52,56},{60,64},{68,... | collective-permute-start | bytes 442376 | tf_op jit(solution)/shard_map/ppermute | solution.py:334
  10.4 4.1 %collective-permute-start.2 = (f32[2,16,1024]{2,1,0:T(8,128)S(1)}, f32[2,16,1024]{2,1,0:T(8,128)S(1)}, u32[]{:S(2)}, u32[]{:S(2)}) collective-permute-start(f32[2,16,1024]{2,1,0:T(8,128)S(1)} %slice_bitcast_fusion), channel_id=1, source_target_pairs={{0,1},{1,0},{2,3},{3,2},{4,5},{5,4},{6,7},{7,6},{8,9},{9,8},{10,11... | collective-permute-start | bytes 393224 | tf_op jit(solution)/shard_map/ppermute | solution.py:338
  15.2 20.0 %collective-permute-start.3 = (f32[2,2,16,1024]{3,2,1,0:T(8,128)S(1)}, f32[2,2,16,1024]{3,2,1,0:T(8,128)S(1)}, u32[]{:S(2)}, u32[]{:S(2)}) collective-permute-start(f32[2,2,16,1024]{3,2,1,0:T(8,128)S(1)} %get-tuple-element.20.ours_ref), channel_id=1, source_target_pairs={{0,2},{2,0},{1,3},{3,1},{4,6},{6,4},{5,7},{7,5},{8,10},{10,8},{9,1... | collective-permute-start | bytes 786440 | tf_op jit(solution)/shard_map/ppermute | solution.py:338
  20.8 4.9 %collective-permute-start.4 = (f32[1,2,16,1024]{3,2,1,0:T(8,128)S(1)}, f32[1,2,16,1024]{3,2,1,0:T(8,128)S(1)}, u32[]{:S(2)}, u32[]{:S(2)}) collective-permute-start(f32[1,2,16,1024]{3,2,1,0:T(8,128)S(1)} %slice.20), channel_id=1, source_target_pairs={{0,1},{1,0},{2,3},{3,2},{4,5},{5,4},{6,7},{7,6},{8,9},{9,8},{10,11... | collective-permute-start | bytes 393224 | tf_op jit(solution)/shard_map/ppermute | solution.py:338
  25.8 20.0 %collective-permute-start.5 = (f32[2,1,16,1024]{3,2,1,0:T(8,128)S(1)}, f32[2,1,16,1024]{3,2,1,0:T(8,128)S(1)}, u32[]{:S(2)}, u32[]{:S(2)}) collective-permute-start(f32[2,1,16,1024]{3,2,1,0:T(8,128)S(1)} %pad_maximum_fusion.rest_0_.ours_ref), channel_id=1, source_target_pairs={{0,2},{2,0},{1,3},{3,1},{4,6},{6,4},{5,7},{7,5},{8,10},{10,8},{9,1... | collective-permute-start | bytes 393224 | tf_op jit(solution)/shard_map/ppermute | solution.py:338
  28.4 20.2 %collective-permute-start.6 = (f32[2,1,16,1024]{3,2,1,0:T(8,128)S(1)}, f32[2,1,16,1024]{3,2,1,0:T(8,128)S(1)}, u32[]{:S(2)}, u32[]{:S(2)}) collective-permute-start(f32[2,1,16,1024]{3,2,1,0:T(8,128)S(1)} %pad_maximum_fusion.1.rest_1_.ours_ref), channel_id=1, source_target_pairs={{0,2},{2,0},{1,3},{3,1},{4,6},{6,4},{5,7},{7,5},{8,10},{10,8},{9,1... | collective-permute-start | bytes 393224 | tf_op jit(solution)/shard_map/ppermute | solution.py:338
  51.1 3.8 %collective-permute-start.7 = (f32[4,16,1024]{2,1,0:T(8,128)S(1)}, f32[4,16,1024]{2,1,0:T(8,128)S(1)}, u32[]{:S(2)}, u32[]{:S(2)}) collective-permute-start(f32[4,16,1024]{2,1,0:T(8,128)S(1)} %get-tuple-element.30), channel_id=1, source_target_pairs={{0,1},{1,0},{2,3},{3,2},{4,5},{5,4},{6,7},{7,6},{8,9},{9,8},{10,11... | collective-permute-start | bytes 786440 | tf_op jit(solution)/shard_map/ppermute | solution.py:338

commit v4 on v3

--- a/solution.py
+++ b/solution.py
@@ -55,7 +55,7 @@
     return jax.ShapeDtypeStruct(shape, jnp.float32)
 
 
-def table_kernel(levels_ref, target_ref, weights_ref, rate_ref, all_ref, own_ref, linear_ref):
+def table_kernel(levels_ref, target_ref, weights_ref, rate_ref, _, all_ref, own_ref, linear_ref):
     far = lax.axis_index("far")
     levels = levels_ref[...].astype(jnp.float32)
     row = lax.broadcasted_iota(jnp.int32, (NC, NC), 0)
@@ -91,7 +91,7 @@
     linear_ref[...] = jnp.concatenate([high, high, low, low], 1)
 
 
-def make_tables(kernel_levels, pair_target, fragment_weights, breakage_rate):
+def make_tables(kernel_levels, pair_target, fragment_weights, breakage_rate, after):
     bf16 = jnp.bfloat16
     return call(
         table_kernel,
@@ -101,7 +101,9 @@
             jax.ShapeDtypeStruct((NC, 4 * NC), bf16),
         ),
         "tables",
-    )(kernel_levels, pair_target, fragment_weights, breakage_rate.reshape(1, NC))
+        in_specs=[pl.BlockSpec(memory_space=pltpu.VMEM)] * 4
+        + [pl.BlockSpec(memory_space=pl.ANY)],
+    )(kernel_levels, pair_target, fragment_weights, breakage_rate.reshape(1, NC), after)
 
 
 def column(settling):
@@ -377,11 +379,13 @@
         in_specs=[pl.BlockSpec(memory_space=pltpu.HBM)] * 4,
     )(*placed)
     peer = swapped(inner[1], "near")
-    tables = make_tables(kernel_levels, pair_target, fragment_weights, breakage_rate)
     outer, inner = call(outer_kernel, (halves, halves), "outer", cost=1_000_000_000)(
         *local, from_even, from_odd, inner, peer
     )
     inner_far = swapped(inner, "far")
+    tables = make_tables(
+        kernel_levels, pair_target, fragment_weights, breakage_rate, outer
+    )
     outer_peer = swapped(outer[1:], "near")
     ours = [jnp.concatenate([outer[:1, k : k + 1], outer_peer[:, k : k + 1]], 0) for k in range(2)]
     theirs = [swapped(x, "far") for x in ours]

time: 56.2 us -> 56.1 us (level); the launches traced: 55.8 us -> 55.1 us
  waiting for transfers between devices: 8.22 us -> 5.69 us
  starting transfers between devices: 32.3 us -> 34.1 us
    ppermute x6, waiting for transfers between devices: 8.22 us -> 5.68 us  [swapped(): return lax.ppermute(x, axis, [(0, 1), (1, 0)])]
    ppermute x6, starting transfers between devices: 24.7 us -> 26.6 us  [swapped(): return lax.ppermute(x, axis, [(0, 1), (1, 0)])]
  transfers between devices with their start and end apart: 8 -> 8, of which waited for: 5 -> 4; matrix products, arithmetic and copies ran while one was open for 0% -> 0% of each run, Pallas kernels for 17% -> 18%
where the time goes in v4:
time: 56.1 us; the launch traced here: 55.1 us
  starting transfers between devices  34.1 us (61%)
  Pallas kernels  14.9 us (27%)
  waiting for transfers between devices  5.69 us (10%)
    ppermute x6, starting transfers between devices, swapped(): return lax.ppermute(x, axis, [(0, 1), (1, 0)])  26.6 us
    pallas_call x3, Pallas kernels, react(): call(react_kernel, (f32(layers, GROUP, WIDTH), f32(sent, GROUP, WIDTH)),...  9.99 us
    ppermute x2, starting transfers between devices, swapped_in_pairs(): return lax.ppermute(x, 'tile', pairs + [(b, a) for a, b in pairs])  7.57 us
    ppermute x6, waiting for transfers between devices, swapped(): return lax.ppermute(x, axis, [(0, 1), (1, 0)])  5.68 us
    pallas_call x1, Pallas kernels, body(): call(inner_kernel, halves, 'inner', scratch=[pltpu.VMEM(x.shape, x.dtype)...  1.59 us
  transfers between devices with their start and end apart: 8, of which 4 were waited for; matrix products, arithmetic and copies ran while one was open for 0% of the time, Pallas kernels for 18%

profile of v4, /device:TPU:7, one launch (start us, length us, event | category | flops | bytes accessed | tf_op | source)
XLA Modules:
  0.0 55.1 jit_solution(14186055506682995802)
XLA Ops:
  0.0 0.0 copy-start.6
  0.0 1.1 %edges.1 = (f32[18,4,512]{2,1,0:T(4,128)S(1)}, f32[18,4,512]{2,1,0:T(4,128)S(1)}) custom-call(f32[16,4,2048]{2,1,0:T(4,128)} %c_ref.3, f32[2,4,2048]{2,1,0:T(4,128)} %velocity_ref.3, s32[16,128]{1,0:T(8,128)} %bitcast.5), custom_call_target="tpu_custom_call" | custom-call | tf_op jit(solution)/shard_map/edges/pallas_call | solution.py:362
  1.1 3.2 %collective-permute-start = (f32[18,4,512]{2,1,0:T(4,128)S(1)}, f32[18,4,512]{2,1,0:T(4,128)S(1)}, u32[]{:S(2)}, u32[]{:S(2)}) collective-permute-start(f32[18,4,512]{2,1,0:T(4,128)S(1)} %get-tuple-element.18), channel_id=1, source_target_pairs={{0,4},{8,12},{16,20},{24,28},{32,36},{40,44},{48,52},{56,60},{64,6... | collective-permute-start | bytes 442376 | tf_op jit(solution)/shard_map/ppermute | solution.py:336
  4.3 4.4 %collective-permute-start.1 = (f32[18,4,512]{2,1,0:T(4,128)S(1)}, f32[18,4,512]{2,1,0:T(4,128)S(1)}, u32[]{:S(2)}, u32[]{:S(2)}) collective-permute-start(f32[18,4,512]{2,1,0:T(4,128)S(1)} %get-tuple-element.19), channel_id=1, source_target_pairs={{4,8},{12,16},{20,24},{28,32},{36,40},{44,48},{52,56},{60,64},{68,... | collective-permute-start | bytes 442376 | tf_op jit(solution)/shard_map/ppermute | solution.py:336
  8.7 1.6 %inner.1.inner_ref = f32[2,2,16,1024]{3,2,1,0:T(8,128)S(1)} custom-call(f32[16,4,2048]{2,1,0:T(4,128)} %c_ref.3, f32[2,4,2048]{2,1,0:T(4,128)} %velocity_ref.3, s32[16,128]{1,0:T(8,128)} %bitcast.6, f32[1,16]{1,0:T(1,128)} %bitcast.8), custom_call_target="tpu_custom_call" | custom-call | tf_op jit(solution)/shard_map/inner/pallas_call | solution.py:374
  10.3 0.0 copy-start.3
  10.4 0.0 copy-start.5
  10.4 0.0 copy-start.7
  10.4 3.3 %collective-permute-start.2 = (f32[2,16,1024]{2,1,0:T(8,128)S(1)}, f32[2,16,1024]{2,1,0:T(8,128)S(1)}, u32[]{:S(2)}, u32[]{:S(2)}) collective-permute-start(f32[2,16,1024]{2,1,0:T(8,128)S(1)} %slice_bitcast_fusion), channel_id=1, source_target_pairs={{0,1},{1,0},{2,3},{3,2},{4,5},{5,4},{6,7},{7,6},{8,9},{9,8},{10,11... | collective-permute-start | bytes 393224 | tf_op jit(solution)/shard_map/ppermute | solution.py:340
  13.7 1.0 %collective-permute-done.2.peer_ref = f32[2,16,1024]{2,1,0:T(8,128)S(1)} collective-permute-done((f32[2,16,1024]{2,1,0:T(8,128)S(1)}, f32[2,16,1024]{2,1,0:T(8,128)S(1)}, u32[]{:S(2)}, u32[]{:S(2)}) %collective-permute-start.2) | collective-permute-done | bytes 131104 | tf_op jit(solution)/shard_map/ppermute | solution.py:340
  14.7 0.6 %outer.1 = (f32[2,2,16,1024]{3,2,1,0:T(8,128)S(1)}, f32[2,2,16,1024]{3,2,1,0:T(8,128)S(1)}) custom-call(f32[16,4,2048]{2,1,0:T(4,128)S(1)} %copy-done, f32[2,4,2048]{2,1,0:T(4,128)S(1)} %copy-done.1, s32[16,128]{1,0:T(8,128)S(1)} %bitcast.7, f32[1,16]{1,0:T(1,128)S(1)} %bitcast.9, f32[18,4,512]{2,1,0:T(4,128)S(1)} %collective-permute-done.even_ref, ...), custom_call_target="tpu_custom_call" | custom-call | flops 1000000000 | tf_op jit(solution)/shard_map/outer/pallas_call | solution.py:382
  15.3 5.7 %collective-permute-start.3 = (f32[2,2,16,1024]{3,2,1,0:T(8,128)S(1)}, f32[2,2,16,1024]{3,2,1,0:T(8,128)S(1)}, u32[]{:S(2)}, u32[]{:S(2)}) collective-permute-start(f32[2,2,16,1024]{3,2,1,0:T(8,128)S(1)} %get-tuple-element.20.ours_ref), channel_id=1, source_target_pairs={{0,2},{2,0},{1,3},{3,1},{4,6},{6,4},{5,7},{7,5},{8,10},{10,8},{9,1... | collective-permute-start | bytes 786440 | tf_op jit(solution)/shard_map/ppermute | solution.py:340
  21.0 3.7 %collective-permute-start.4 = (f32[1,2,16,1024]{3,2,1,0:T(8,128)S(1)}, f32[1,2,16,1024]{3,2,1,0:T(8,128)S(1)}, u32[]{:S(2)}, u32[]{:S(2)}) collective-permute-start(f32[1,2,16,1024]{3,2,1,0:T(8,128)S(1)} %slice.20), channel_id=1, source_target_pairs={{0,1},{1,0},{2,3},{3,2},{4,5},{5,4},{6,7},{7,6},{8,9},{9,8},{10,11... | collective-permute-start | bytes 393224 | tf_op jit(solution)/shard_map/ppermute | solution.py:340
  24.8 0.7 %tables.1 = (bf16[2304,256]{1,0:T(8,128)(2,1)S(1)}, bf16[1664,256]{1,0:T(8,128)(2,1)S(1)}, bf16[64,256]{1,0:T(8,128)(2,1)S(1)}) custom-call(s32[64,64]{1,0:T(8,128)S(1)} %copy-done.3, s32[64,64]{1,0:T(8,128)S(1)} %copy-done.4, s32[64,64]{1,0:T(8,128)S(1)} %copy-done.5, f32[1,64]{1,0:T(1,128)S(1)} %bitcast.10, f32[2,2,16,1024]{3,2,1,0:T(8,128)S(1)} %get-tuple-element.21._), custom_call_target="tpu_custom_call" | custom-call | tf_op jit(solution)/shard_map/tables/pallas_call | solution.py:96
  25.5 0.2 collective-permute-done.4
  25.7 2.6 %collective-permute-start.5 = (f32[2,1,16,1024]{3,2,1,0:T(8,128)S(1)}, f32[2,1,16,1024]{3,2,1,0:T(8,128)S(1)}, u32[]{:S(2)}, u32[]{:S(2)}) collective-permute-start(f32[2,1,16,1024]{3,2,1,0:T(8,128)S(1)} %pad_maximum_fusion.rest_0_.ours_ref), channel_id=1, source_target_pairs={{0,2},{2,0},{1,3},{3,1},{4,6},{6,4},{5,7},{7,5},{8,10},{10,8},{9,1... | collective-permute-start | bytes 393224 | tf_op jit(solution)/shard_map/ppermute | solution.py:340
  28.4 6.7 %collective-permute-start.6 = (f32[2,1,16,1024]{3,2,1,0:T(8,128)S(1)}, f32[2,1,16,1024]{3,2,1,0:T(8,128)S(1)}, u32[]{:S(2)}, u32[]{:S(2)}) collective-permute-start(f32[2,1,16,1024]{3,2,1,0:T(8,128)S(1)} %pad_maximum_fusion.1.rest_1_.ours_ref), channel_id=1, source_target_pairs={{0,2},{2,0},{1,3},{3,1},{4,6},{6,4},{5,7},{7,5},{8,10},{10,8},{9,1... | collective-permute-start | bytes 393224 | tf_op jit(solution)/shard_map/ppermute | solution.py:340
  35.1 4.9 %react.3 = (f32[2,16,1024]{2,1,0:T(8,128)S(1)}, f32[2,16,1024]{2,1,0:T(8,128)S(1)}) custom-call(f32[2,2,16,1024]{3,2,1,0:T(8,128)S(1)} %get-tuple-element.20.ours_ref, f32[2,2,16,1024]{3,2,1,0:T(8,128)S(1)} %collective-permute-done.3.theirs_ref, bf16[2304,256]{1,0:T(8,128)(2,1)S(1)} %get-tuple-element.22.all_ref, ...), custom_call_target="tpu_custom_call" | custom-call | flops 6000000000 | tf_op jit(solution)/shard_map/react/pallas_call | solution.py:311
  40.0 2.6 %react.4 = (f32[1,16,1024]{2,1,0:T(8,128)S(1)}, f32[1,16,1024]{2,1,0:T(8,128)S(1)}) custom-call(f32[2,1,16,1024]{3,2,1,0:T(8,128)S(1)} %pad_maximum_fusion.rest_0_.ours_ref, f32[2,1,16,1024]{3,2,1,0:T(8,128)S(1)} %collective-permute-done.5.theirs_ref, bf16[2304,256]{1,0:T(8,128)(2,1)S(1)} %get-tuple-element.22.all_ref, ...), custom_call_target="tpu_custom_call" | custom-call | flops 3000000000 | tf_op jit(solution)/shard_map/react/pallas_call | solution.py:311
  42.6 3.4 %collective-permute-done.6.theirs_ref = f32[2,1,16,1024]{3,2,1,0:T(8,128)S(1)} collective-permute-done((f32[2,1,16,1024]{3,2,1,0:T(8,128)S(1)}, f32[2,1,16,1024]{3,2,1,0:T(8,128)S(1)}, u32[]{:S(2)}, u32[]{:S(2)}) %collective-permute-start.6) | collective-permute-done | bytes 131104 | tf_op jit(solution)/shard_map/ppermute | solution.py:340
  46.0 2.6 %react.5 = (f32[1,16,1024]{2,1,0:T(8,128)S(1)}, f32[4,16,1024]{2,1,0:T(8,128)S(1)}) custom-call(f32[2,1,16,1024]{3,2,1,0:T(8,128)S(1)} %pad_maximum_fusion.1.rest_1_.ours_ref, f32[2,1,16,1024]{3,2,1,0:T(8,128)S(1)} %collective-permute-done.6.theirs_ref, bf16[2304,256]{1,0:T(8,128)(2,1)S(1)} %get-tuple-element.22.all_ref, ...), custom_call_target="tpu_custom_call" | custom-call | flops 3000000000 | tf_op jit(solution)/shard_map/react/pallas_call | solution.py:311
  48.6 4.5 %collective-permute-start.7 = (f32[4,16,1024]{2,1,0:T(8,128)S(1)}, f32[4,16,1024]{2,1,0:T(8,128)S(1)}, u32[]{:S(2)}, u32[]{:S(2)}) collective-permute-start(f32[4,16,1024]{2,1,0:T(8,128)S(1)} %get-tuple-element.30), channel_id=1, source_target_pairs={{0,1},{1,0},{2,3},{3,2},{4,5},{5,4},{6,7},{7,6},{8,9},{9,8},{10,11... | collective-permute-start | bytes 786440 | tf_op jit(solution)/shard_map/ppermute | solution.py:340
  53.1 1.1 %collective-permute-done.7.peer_ref = f32[4,16,1024]{2,1,0:T(8,128)S(1)} collective-permute-done((f32[4,16,1024]{2,1,0:T(8,128)S(1)}, f32[4,16,1024]{2,1,0:T(8,128)S(1)}, u32[]{:S(2)}, u32[]{:S(2)}) %collective-permute-start.7) | collective-permute-done | bytes 262176 | tf_op jit(solution)/shard_map/ppermute | solution.py:340
  54.2 0.9 %lay.1 = f32[16,4,2048]{2,1,0:T(4,128)} custom-call(f32[2,16,1024]{2,1,0:T(8,128)S(1)} %get-tuple-element.25.inner_ref, f32[1,16,1024]{2,1,0:T(8,128)S(1)} %get-tuple-element.26.first_ref, f32[1,16,1024]{2,1,0:T(8,128)S(1)} %get-tuple-element.29.second_ref, f32[4,16,1024]{2,1,0:T(8,128)S(1)} %collective-permute-done.7.peer_ref), custom_call_target="tpu_custom_call" | custom-call | tf_op jit(solution)/shard_map/lay/pallas_call | solution.py:396
  (22 shorter events, 0.1 us)
Async XLA Ops:
  0.0 14.6 %copy-start = (f32[16,4,2048]{2,1,0:T(4,128)S(1)}, f32[16,4,2048]{2,1,0:T(4,128)}, u32[]{:S(2)}) copy-start(f32[16,4,2048]{2,1,0:T(4,128)} %c_ref.3) | copy-start | bytes 1572868
  0.0 14.6 %copy-start.1 = (f32[2,4,2048]{2,1,0:T(4,128)S(1)}, f32[2,4,2048]{2,1,0:T(4,128)}, u32[]{:S(2)}) copy-start(f32[2,4,2048]{2,1,0:T(4,128)} %velocity_ref.3) | copy-start | bytes 196612
  0.0 14.7 %copy-start.2 = (s32[2048]{0:T(1024)S(1)}, s32[2048]{0:T(1024)}, u32[]{:S(2)}) copy-start(s32[2048]{0:T(1024)} %param.10) | copy-start | bytes 24580
  0.0 14.7 %copy-start.6 = (f32[16]{0:T(128)S(1)}, f32[16]{0:T(128)}, u32[]{:S(2)}) copy-start(f32[16]{0:T(128)} %param.11) | copy-start | bytes 196
  1.1 13.5 %collective-permute-start = (f32[18,4,512]{2,1,0:T(4,128)S(1)}, f32[18,4,512]{2,1,0:T(4,128)S(1)}, u32[]{:S(2)}, u32[]{:S(2)}) collective-permute-start(f32[18,4,512]{2,1,0:T(4,128)S(1)} %get-tuple-element.18), channel_id=1, source_target_pairs={{0,4},{8,12},{16,20},{24,28},{32,36},{40,44},{48,52},{56,60},{64,6... | collective-permute-start | bytes 442376 | tf_op jit(solution)/shard_map/ppermute | solution.py:336
  4.3 10.3 %collective-permute-start.1 = (f32[18,4,512]{2,1,0:T(4,128)S(1)}, f32[18,4,512]{2,1,0:T(4,128)S(1)}, u32[]{:S(2)}, u32[]{:S(2)}) collective-permute-start(f32[18,4,512]{2,1,0:T(4,128)S(1)} %get-tuple-element.19), channel_id=1, source_target_pairs={{4,8},{12,16},{20,24},{28,32},{36,40},{44,48},{52,56},{60,64},{68,... | collective-permute-start | bytes 442376 | tf_op jit(solution)/shard_map/ppermute | solution.py:336
  10.3 14.4 %copy-start.3 = (s32[64,64]{1,0:T(8,128)S(1)}, s32[64,64]{1,0:T(8,128)}, u32[]{:S(2)}) copy-start(s32[64,64]{1,0:T(8,128)} %levels_ref.1) | copy-start | bytes 49156
  10.4 14.4 %copy-start.4 = (s32[64,64]{1,0:T(8,128)S(1)}, s32[64,64]{1,0:T(8,128)}, u32[]{:S(2)}) copy-start(s32[64,64]{1,0:T(8,128)} %target_ref.1) | copy-start | bytes 49156
  10.4 14.4 %copy-start.5 = (s32[64,64]{1,0:T(8,128)S(1)}, s32[64,64]{1,0:T(8,128)}, u32[]{:S(2)}) copy-start(s32[64,64]{1,0:T(8,128)} %weights_ref.1) | copy-start | bytes 49156
  10.4 14.4 %copy-start.7 = (f32[64]{0:T(128)S(1)}, f32[64]{0:T(128)}, u32[]{:S(2)}) copy-start(f32[64]{0:T(128)} %param.12) | copy-start | bytes 772
  10.4 4.2 %collective-permute-start.2 = (f32[2,16,1024]{2,1,0:T(8,128)S(1)}, f32[2,16,1024]{2,1,0:T(8,128)S(1)}, u32[]{:S(2)}, u32[]{:S(2)}) collective-permute-start(f32[2,16,1024]{2,1,0:T(8,128)S(1)} %slice_bitcast_fusion), channel_id=1, source_target_pairs={{0,1},{1,0},{2,3},{3,2},{4,5},{5,4},{6,7},{7,6},{8,9},{9,8},{10,11... | collective-permute-start | bytes 393224 | tf_op jit(solution)/shard_map/ppermute | solution.py:340
  15.3 19.8 %collective-permute-start.3 = (f32[2,2,16,1024]{3,2,1,0:T(8,128)S(1)}, f32[2,2,16,1024]{3,2,1,0:T(8,128)S(1)}, u32[]{:S(2)}, u32[]{:S(2)}) collective-permute-start(f32[2,2,16,1024]{3,2,1,0:T(8,128)S(1)} %get-tuple-element.20.ours_ref), channel_id=1, source_target_pairs={{0,2},{2,0},{1,3},{3,1},{4,6},{6,4},{5,7},{7,5},{8,10},{10,8},{9,1... | collective-permute-start | bytes 786440 | tf_op jit(solution)/shard_map/ppermute | solution.py:340
  21.0 4.7 %collective-permute-start.4 = (f32[1,2,16,1024]{3,2,1,0:T(8,128)S(1)}, f32[1,2,16,1024]{3,2,1,0:T(8,128)S(1)}, u32[]{:S(2)}, u32[]{:S(2)}) collective-permute-start(f32[1,2,16,1024]{3,2,1,0:T(8,128)S(1)} %slice.20), channel_id=1, source_target_pairs={{0,1},{1,0},{2,3},{3,2},{4,5},{5,4},{6,7},{7,6},{8,9},{9,8},{10,11... | collective-permute-start | bytes 393224 | tf_op jit(solution)/shard_map/ppermute | solution.py:340
  25.7 14.3 %collective-permute-start.5 = (f32[2,1,16,1024]{3,2,1,0:T(8,128)S(1)}, f32[2,1,16,1024]{3,2,1,0:T(8,128)S(1)}, u32[]{:S(2)}, u32[]{:S(2)}) collective-permute-start(f32[2,1,16,1024]{3,2,1,0:T(8,128)S(1)} %pad_maximum_fusion.rest_0_.ours_ref), channel_id=1, source_target_pairs={{0,2},{2,0},{1,3},{3,1},{4,6},{6,4},{5,7},{7,5},{8,10},{10,8},{9,1... | collective-permute-start | bytes 393224 | tf_op jit(solution)/shard_map/ppermute | solution.py:340
  28.4 17.6 %collective-permute-start.6 = (f32[2,1,16,1024]{3,2,1,0:T(8,128)S(1)}, f32[2,1,16,1024]{3,2,1,0:T(8,128)S(1)}, u32[]{:S(2)}, u32[]{:S(2)}) collective-permute-start(f32[2,1,16,1024]{3,2,1,0:T(8,128)S(1)} %pad_maximum_fusion.1.rest_1_.ours_ref), channel_id=1, source_target_pairs={{0,2},{2,0},{1,3},{3,1},{4,6},{6,4},{5,7},{7,5},{8,10},{10,8},{9,1... | collective-permute-start | bytes 393224 | tf_op jit(solution)/shard_map/ppermute | solution.py:340
  48.6 5.7 %collective-permute-start.7 = (f32[4,16,1024]{2,1,0:T(8,128)S(1)}, f32[4,16,1024]{2,1,0:T(8,128)S(1)}, u32[]{:S(2)}, u32[]{:S(2)}) collective-permute-start(f32[4,16,1024]{2,1,0:T(8,128)S(1)} %get-tuple-element.30), channel_id=1, source_target_pairs={{0,1},{1,0},{2,3},{3,2},{4,5},{5,4},{6,7},{7,6},{8,9},{9,8},{10,11... | collective-permute-start | bytes 786440 | tf_op jit(solution)/shard_map/ppermute | solution.py:340

commit v5 on v3

--- a/solution.py
+++ b/solution.py
@@ -15,7 +15,7 @@
 WIDTH = 2 * CY
 TILE = 512
 LANES = 4
-DOTS = [[0, 1], [2, 3], [4, 5, 6, 7]]
+DOTS = [[0, 1, 2, 3], [4, 5, 6, 7]]
 HALF_SCALE = 0.5e-05
 VMEM_LIMIT = 48 * 1024 * 1024
 

time: 56.2 us -> 56.1 us (level)
  no operation moved by 1% of the time
where the time goes in v5:
time: 56.1 us; the launch traced here: 55.8 us
  starting transfers between devices  32.3 us (58%)
  Pallas kernels  14.9 us (27%)
  waiting for transfers between devices  8.23 us (15%)
    ppermute x6, starting transfers between devices, swapped(): return lax.ppermute(x, axis, [(0, 1), (1, 0)])  24.7 us
    pallas_call x3, Pallas kernels, react(): call(react_kernel, (f32(layers, GROUP, WIDTH), f32(sent, GROUP, WIDTH)),...  9.98 us
    ppermute x6, waiting for transfers between devices, swapped(): return lax.ppermute(x, axis, [(0, 1), (1, 0)])  8.23 us
    ppermute x2, starting transfers between devices, swapped_in_pairs(): return lax.ppermute(x, 'tile', pairs + [(b, a) for a, b in pairs])  7.57 us
    pallas_call x1, Pallas kernels, body(): call(inner_kernel, halves, 'inner', scratch=[pltpu.VMEM(x.shape, x.dtype)...  1.59 us
  transfers between devices with their start and end apart: 8, of which 5 were waited for; matrix products, arithmetic and copies ran while one was open for 0% of the time, Pallas kernels for 17%

profile of v5, /device:TPU:7, one launch (start us, length us, event | category | flops | bytes accessed | tf_op | source)
XLA Modules:
  0.0 55.8 jit_solution(17721725010666316634)
XLA Ops:
  0.0 0.0 copy-start.7
  0.1 1.1 %edges.1 = (f32[18,4,512]{2,1,0:T(4,128)S(1)}, f32[18,4,512]{2,1,0:T(4,128)S(1)}) custom-call(f32[16,4,2048]{2,1,0:T(4,128)} %c_ref.3, f32[2,4,2048]{2,1,0:T(4,128)} %velocity_ref.3, s32[16,128]{1,0:T(8,128)} %bitcast.5), custom_call_target="tpu_custom_call" | custom-call | tf_op jit(solution)/shard_map/edges/pallas_call | solution.py:360
  1.2 3.2 %collective-permute-start = (f32[18,4,512]{2,1,0:T(4,128)S(1)}, f32[18,4,512]{2,1,0:T(4,128)S(1)}, u32[]{:S(2)}, u32[]{:S(2)}) collective-permute-start(f32[18,4,512]{2,1,0:T(4,128)S(1)} %get-tuple-element.18), channel_id=1, source_target_pairs={{0,4},{8,12},{16,20},{24,28},{32,36},{40,44},{48,52},{56,60},{64,6... | collective-permute-start | bytes 442376 | tf_op jit(solution)/shard_map/ppermute | solution.py:334
  4.4 4.4 %collective-permute-start.1 = (f32[18,4,512]{2,1,0:T(4,128)S(1)}, f32[18,4,512]{2,1,0:T(4,128)S(1)}, u32[]{:S(2)}, u32[]{:S(2)}) collective-permute-start(f32[18,4,512]{2,1,0:T(4,128)S(1)} %get-tuple-element.19), channel_id=1, source_target_pairs={{4,8},{12,16},{20,24},{28,32},{36,40},{44,48},{52,56},{60,64},{68,... | collective-permute-start | bytes 442376 | tf_op jit(solution)/shard_map/ppermute | solution.py:334
  8.8 1.6 %inner.1.inner_ref = f32[2,2,16,1024]{3,2,1,0:T(8,128)S(1)} custom-call(f32[16,4,2048]{2,1,0:T(4,128)} %c_ref.3, f32[2,4,2048]{2,1,0:T(4,128)} %velocity_ref.3, s32[16,128]{1,0:T(8,128)} %bitcast.6, f32[1,16]{1,0:T(1,128)} %bitcast.9), custom_call_target="tpu_custom_call" | custom-call | tf_op jit(solution)/shard_map/inner/pallas_call | solution.py:372
  10.4 3.1 %collective-permute-start.2 = (f32[2,16,1024]{2,1,0:T(8,128)S(1)}, f32[2,16,1024]{2,1,0:T(8,128)S(1)}, u32[]{:S(2)}, u32[]{:S(2)}) collective-permute-start(f32[2,16,1024]{2,1,0:T(8,128)S(1)} %slice_bitcast_fusion), channel_id=1, source_target_pairs={{0,1},{1,0},{2,3},{3,2},{4,5},{5,4},{6,7},{7,6},{8,9},{9,8},{10,11... | collective-permute-start | bytes 393224 | tf_op jit(solution)/shard_map/ppermute | solution.py:338
  13.6 0.7 %tables.1 = (bf16[2304,256]{1,0:T(8,128)(2,1)S(1)}, bf16[1664,256]{1,0:T(8,128)(2,1)S(1)}, bf16[64,256]{1,0:T(8,128)(2,1)S(1)}) custom-call(s32[64,64]{1,0:T(8,128)S(1)} %copy-done.3, s32[64,64]{1,0:T(8,128)S(1)} %copy-done.4, s32[64,64]{1,0:T(8,128)S(1)} %copy-done.5, f32[1,64]{1,0:T(1,128)S(1)} %bitcast.8), custom_call_target="tpu_custom_call" | custom-call | tf_op jit(solution)/shard_map/tables/pallas_call | solution.py:96
  14.3 0.2 collective-permute-done.2.peer_ref
  14.5 0.0 collective-permute-done.even_ref
  14.5 0.0 collective-permute-done.1.odd_ref
  14.5 0.6 %outer.1 = (f32[2,2,16,1024]{3,2,1,0:T(8,128)S(1)}, f32[2,2,16,1024]{3,2,1,0:T(8,128)S(1)}) custom-call(f32[16,4,2048]{2,1,0:T(4,128)S(1)} %copy-done, f32[2,4,2048]{2,1,0:T(4,128)S(1)} %copy-done.1, s32[16,128]{1,0:T(8,128)S(1)} %bitcast.7, f32[1,16]{1,0:T(1,128)S(1)} %bitcast.10, f32[18,4,512]{2,1,0:T(4,128)S(1)} %collective-permute-done.even_ref, ...), custom_call_target="tpu_custom_call" | custom-call | flops 1000000000 | tf_op jit(solution)/shard_map/outer/pallas_call | solution.py:381
  15.2 5.7 %collective-permute-start.3 = (f32[2,2,16,1024]{3,2,1,0:T(8,128)S(1)}, f32[2,2,16,1024]{3,2,1,0:T(8,128)S(1)}, u32[]{:S(2)}, u32[]{:S(2)}) collective-permute-start(f32[2,2,16,1024]{3,2,1,0:T(8,128)S(1)} %get-tuple-element.20.ours_ref), channel_id=1, source_target_pairs={{0,2},{2,0},{1,3},{3,1},{4,6},{6,4},{5,7},{7,5},{8,10},{10,8},{9,1... | collective-permute-start | bytes 786440 | tf_op jit(solution)/shard_map/ppermute | solution.py:338
  20.8 3.9 %collective-permute-start.4 = (f32[1,2,16,1024]{3,2,1,0:T(8,128)S(1)}, f32[1,2,16,1024]{3,2,1,0:T(8,128)S(1)}, u32[]{:S(2)}, u32[]{:S(2)}) collective-permute-start(f32[1,2,16,1024]{3,2,1,0:T(8,128)S(1)} %slice.20), channel_id=1, source_target_pairs={{0,1},{1,0},{2,3},{3,2},{4,5},{5,4},{6,7},{7,6},{8,9},{9,8},{10,11... | collective-permute-start | bytes 393224 | tf_op jit(solution)/shard_map/ppermute | solution.py:338
  24.8 0.9 %collective-permute-done.4 = f32[1,2,16,1024]{3,2,1,0:T(8,128)S(1)} collective-permute-done((f32[1,2,16,1024]{3,2,1,0:T(8,128)S(1)}, f32[1,2,16,1024]{3,2,1,0:T(8,128)S(1)}, u32[]{:S(2)}, u32[]{:S(2)}) %collective-permute-start.4) | collective-permute-done | bytes 131104 | tf_op jit(solution)/shard_map/ppermute | solution.py:338
  25.8 2.6 %collective-permute-start.5 = (f32[2,1,16,1024]{3,2,1,0:T(8,128)S(1)}, f32[2,1,16,1024]{3,2,1,0:T(8,128)S(1)}, u32[]{:S(2)}, u32[]{:S(2)}) collective-permute-start(f32[2,1,16,1024]{3,2,1,0:T(8,128)S(1)} %pad_maximum_fusion.rest_0_.ours_ref), channel_id=1, source_target_pairs={{0,2},{2,0},{1,3},{3,1},{4,6},{6,4},{5,7},{7,5},{8,10},{10,8},{9,1... | collective-permute-start | bytes 393224 | tf_op jit(solution)/shard_map/ppermute | solution.py:338
  28.4 6.7 %collective-permute-start.6 = (f32[2,1,16,1024]{3,2,1,0:T(8,128)S(1)}, f32[2,1,16,1024]{3,2,1,0:T(8,128)S(1)}, u32[]{:S(2)}, u32[]{:S(2)}) collective-permute-start(f32[2,1,16,1024]{3,2,1,0:T(8,128)S(1)} %pad_maximum_fusion.1.rest_1_.ours_ref), channel_id=1, source_target_pairs={{0,2},{2,0},{1,3},{3,1},{4,6},{6,4},{5,7},{7,5},{8,10},{10,8},{9,1... | collective-permute-start | bytes 393224 | tf_op jit(solution)/shard_map/ppermute | solution.py:338
  35.2 4.9 %react.3 = (f32[2,16,1024]{2,1,0:T(8,128)S(1)}, f32[2,16,1024]{2,1,0:T(8,128)S(1)}) custom-call(f32[2,2,16,1024]{3,2,1,0:T(8,128)S(1)} %get-tuple-element.20.ours_ref, f32[2,2,16,1024]{3,2,1,0:T(8,128)S(1)} %collective-permute-done.3.theirs_ref, bf16[2304,256]{1,0:T(8,128)(2,1)S(1)} %get-tuple-element.21.all_ref, ...), custom_call_target="tpu_custom_call" | custom-call | flops 6000000000 | tf_op jit(solution)/shard_map/react/pallas_call | solution.py:309
  40.1 5.7 %collective-permute-done.5.theirs_ref = f32[2,1,16,1024]{3,2,1,0:T(8,128)S(1)} collective-permute-done((f32[2,1,16,1024]{3,2,1,0:T(8,128)S(1)}, f32[2,1,16,1024]{3,2,1,0:T(8,128)S(1)}, u32[]{:S(2)}, u32[]{:S(2)}) %collective-permute-start.5) | collective-permute-done | bytes 131104 | tf_op jit(solution)/shard_map/ppermute | solution.py:338
  45.8 2.6 %react.4 = (f32[1,16,1024]{2,1,0:T(8,128)S(1)}, f32[1,16,1024]{2,1,0:T(8,128)S(1)}) custom-call(f32[2,1,16,1024]{3,2,1,0:T(8,128)S(1)} %pad_maximum_fusion.rest_0_.ours_ref, f32[2,1,16,1024]{3,2,1,0:T(8,128)S(1)} %collective-permute-done.5.theirs_ref, bf16[2304,256]{1,0:T(8,128)(2,1)S(1)} %get-tuple-element.21.all_ref, ...), custom_call_target="tpu_custom_call" | custom-call | flops 3000000000 | tf_op jit(solution)/shard_map/react/pallas_call | solution.py:309
  48.3 0.2 collective-permute-done.6.theirs_ref
  48.6 2.6 %react.5 = (f32[1,16,1024]{2,1,0:T(8,128)S(1)}, f32[4,16,1024]{2,1,0:T(8,128)S(1)}) custom-call(f32[2,1,16,1024]{3,2,1,0:T(8,128)S(1)} %pad_maximum_fusion.1.rest_1_.ours_ref, f32[2,1,16,1024]{3,2,1,0:T(8,128)S(1)} %collective-permute-done.6.theirs_ref, bf16[2304,256]{1,0:T(8,128)(2,1)S(1)} %get-tuple-element.21.all_ref, ...), custom_call_target="tpu_custom_call" | custom-call | flops 3000000000 | tf_op jit(solution)/shard_map/react/pallas_call | solution.py:309
  51.1 2.6 %collective-permute-start.7 = (f32[4,16,1024]{2,1,0:T(8,128)S(1)}, f32[4,16,1024]{2,1,0:T(8,128)S(1)}, u32[]{:S(2)}, u32[]{:S(2)}) collective-permute-start(f32[4,16,1024]{2,1,0:T(8,128)S(1)} %get-tuple-element.30), channel_id=1, source_target_pairs={{0,1},{1,0},{2,3},{3,2},{4,5},{5,4},{6,7},{7,6},{8,9},{9,8},{10,11... | collective-permute-start | bytes 786440 | tf_op jit(solution)/shard_map/ppermute | solution.py:338
  53.8 1.1 %collective-permute-done.7.peer_ref = f32[4,16,1024]{2,1,0:T(8,128)S(1)} collective-permute-done((f32[4,16,1024]{2,1,0:T(8,128)S(1)}, f32[4,16,1024]{2,1,0:T(8,128)S(1)}, u32[]{:S(2)}, u32[]{:S(2)}) %collective-permute-start.7) | collective-permute-done | bytes 262176 | tf_op jit(solution)/shard_map/ppermute | solution.py:338
  54.9 0.9 %lay.1 = f32[16,4,2048]{2,1,0:T(4,128)} custom-call(f32[2,16,1024]{2,1,0:T(8,128)S(1)} %get-tuple-element.25.inner_ref, f32[1,16,1024]{2,1,0:T(8,128)S(1)} %get-tuple-element.26.first_ref, f32[1,16,1024]{2,1,0:T(8,128)S(1)} %get-tuple-element.29.second_ref, f32[4,16,1024]{2,1,0:T(8,128)S(1)} %collective-permute-done.7.peer_ref), custom_call_target="tpu_custom_call" | custom-call | tf_op jit(solution)/shard_map/lay/pallas_call | solution.py:392
  (22 shorter events, 0.1 us)
Async XLA Ops:
  0.0 14.5 %copy-start = (f32[16,4,2048]{2,1,0:T(4,128)S(1)}, f32[16,4,2048]{2,1,0:T(4,128)}, u32[]{:S(2)}) copy-start(f32[16,4,2048]{2,1,0:T(4,128)} %c_ref.3) | copy-start | bytes 1572868
  0.0 14.5 %copy-start.1 = (f32[2,4,2048]{2,1,0:T(4,128)S(1)}, f32[2,4,2048]{2,1,0:T(4,128)}, u32[]{:S(2)}) copy-start(f32[2,4,2048]{2,1,0:T(4,128)} %velocity_ref.3) | copy-start | bytes 196612
  0.0 14.5 %copy-start.2 = (s32[2048]{0:T(1024)S(1)}, s32[2048]{0:T(1024)}, u32[]{:S(2)}) copy-start(s32[2048]{0:T(1024)} %param.10) | copy-start | bytes 24580
  0.0 14.5 %copy-start.7 = (f32[16]{0:T(128)S(1)}, f32[16]{0:T(128)}, u32[]{:S(2)}) copy-start(f32[16]{0:T(128)} %param.11) | copy-start | bytes 196
  0.0 13.5 %copy-start.3 = (s32[64,64]{1,0:T(8,128)S(1)}, s32[64,64]{1,0:T(8,128)}, u32[]{:S(2)}) copy-start(s32[64,64]{1,0:T(8,128)} %levels_ref.1) | copy-start | bytes 49156
  0.0 13.5 %copy-start.4 = (s32[64,64]{1,0:T(8,128)S(1)}, s32[64,64]{1,0:T(8,128)}, u32[]{:S(2)}) copy-start(s32[64,64]{1,0:T(8,128)} %target_ref.1) | copy-start | bytes 49156
  0.0 13.5 %copy-start.5 = (s32[64,64]{1,0:T(8,128)S(1)}, s32[64,64]{1,0:T(8,128)}, u32[]{:S(2)}) copy-start(s32[64,64]{1,0:T(8,128)} %weights_ref.1) | copy-start | bytes 49156
  0.1 13.5 %copy-start.6 = (f32[64]{0:T(128)S(1)}, f32[64]{0:T(128)}, u32[]{:S(2)}) copy-start(f32[64]{0:T(128)} %param.12) | copy-start | bytes 772
  1.2 13.3 %collective-permute-start = (f32[18,4,512]{2,1,0:T(4,128)S(1)}, f32[18,4,512]{2,1,0:T(4,128)S(1)}, u32[]{:S(2)}, u32[]{:S(2)}) collective-permute-start(f32[18,4,512]{2,1,0:T(4,128)S(1)} %get-tuple-element.18), channel_id=1, source_target_pairs={{0,4},{8,12},{16,20},{24,28},{32,36},{40,44},{48,52},{56,60},{64,6... | collective-permute-start | bytes 442376 | tf_op jit(solution)/shard_map/ppermute | solution.py:334
  4.4 10.1 %collective-permute-start.1 = (f32[18,4,512]{2,1,0:T(4,128)S(1)}, f32[18,4,512]{2,1,0:T(4,128)S(1)}, u32[]{:S(2)}, u32[]{:S(2)}) collective-permute-start(f32[18,4,512]{2,1,0:T(4,128)S(1)} %get-tuple-element.19), channel_id=1, source_target_pairs={{4,8},{12,16},{20,24},{28,32},{36,40},{44,48},{52,56},{60,64},{68,... | collective-permute-start | bytes 442376 | tf_op jit(solution)/shard_map/ppermute | solution.py:334
  10.4 4.1 %collective-permute-start.2 = (f32[2,16,1024]{2,1,0:T(8,128)S(1)}, f32[2,16,1024]{2,1,0:T(8,128)S(1)}, u32[]{:S(2)}, u32[]{:S(2)}) collective-permute-start(f32[2,16,1024]{2,1,0:T(8,128)S(1)} %slice_bitcast_fusion), channel_id=1, source_target_pairs={{0,1},{1,0},{2,3},{3,2},{4,5},{5,4},{6,7},{7,6},{8,9},{9,8},{10,11... | collective-permute-start | bytes 393224 | tf_op jit(solution)/shard_map/ppermute | solution.py:338
  15.2 20.0 %collective-permute-start.3 = (f32[2,2,16,1024]{3,2,1,0:T(8,128)S(1)}, f32[2,2,16,1024]{3,2,1,0:T(8,128)S(1)}, u32[]{:S(2)}, u32[]{:S(2)}) collective-permute-start(f32[2,2,16,1024]{3,2,1,0:T(8,128)S(1)} %get-tuple-element.20.ours_ref), channel_id=1, source_target_pairs={{0,2},{2,0},{1,3},{3,1},{4,6},{6,4},{5,7},{7,5},{8,10},{10,8},{9,1... | collective-permute-start | bytes 786440 | tf_op jit(solution)/shard_map/ppermute | solution.py:338
  20.8 4.9 %collective-permute-start.4 = (f32[1,2,16,1024]{3,2,1,0:T(8,128)S(1)}, f32[1,2,16,1024]{3,2,1,0:T(8,128)S(1)}, u32[]{:S(2)}, u32[]{:S(2)}) collective-permute-start(f32[1,2,16,1024]{3,2,1,0:T(8,128)S(1)} %slice.20), channel_id=1, source_target_pairs={{0,1},{1,0},{2,3},{3,2},{4,5},{5,4},{6,7},{7,6},{8,9},{9,8},{10,11... | collective-permute-start | bytes 393224 | tf_op jit(solution)/shard_map/ppermute | solution.py:338
  25.8 20.0 %collective-permute-start.5 = (f32[2,1,16,1024]{3,2,1,0:T(8,128)S(1)}, f32[2,1,16,1024]{3,2,1,0:T(8,128)S(1)}, u32[]{:S(2)}, u32[]{:S(2)}) collective-permute-start(f32[2,1,16,1024]{3,2,1,0:T(8,128)S(1)} %pad_maximum_fusion.rest_0_.ours_ref), channel_id=1, source_target_pairs={{0,2},{2,0},{1,3},{3,1},{4,6},{6,4},{5,7},{7,5},{8,10},{10,8},{9,1... | collective-permute-start | bytes 393224 | tf_op jit(solution)/shard_map/ppermute | solution.py:338
  28.4 20.2 %collective-permute-start.6 = (f32[2,1,16,1024]{3,2,1,0:T(8,128)S(1)}, f32[2,1,16,1024]{3,2,1,0:T(8,128)S(1)}, u32[]{:S(2)}, u32[]{:S(2)}) collective-permute-start(f32[2,1,16,1024]{3,2,1,0:T(8,128)S(1)} %pad_maximum_fusion.1.rest_1_.ours_ref), channel_id=1, source_target_pairs={{0,2},{2,0},{1,3},{3,1},{4,6},{6,4},{5,7},{7,5},{8,10},{10,8},{9,1... | collective-permute-start | bytes 393224 | tf_op jit(solution)/shard_map/ppermute | solution.py:338
  51.1 3.8 %collective-permute-start.7 = (f32[4,16,1024]{2,1,0:T(8,128)S(1)}, f32[4,16,1024]{2,1,0:T(8,128)S(1)}, u32[]{:S(2)}, u32[]{:S(2)}) collective-permute-start(f32[4,16,1024]{2,1,0:T(8,128)S(1)} %get-tuple-element.30), channel_id=1, source_target_pairs={{0,1},{1,0},{2,3},{3,2},{4,5},{5,4},{6,7},{7,6},{8,9},{9,8},{10,11... | collective-permute-start | bytes 786440 | tf_op jit(solution)/shard_map/ppermute | solution.py:338
